TPU v7x, 256 devices: a whole 4x4x8 slice. The times are simulated.
256 devices in a mesh: lon: 16 (over z, core), lat: 8 (over x_hi, y), lev: 2 (over x_lo).
Axes of the slice: x: 4 (x_hi: 2, x_lo: 2; x = x_hi * 2 + x_lo), y: 4, z: 8, core: 2. Of those that a mesh axis runs over, the one named last changes fastest.
Arguments:
- fields: bfloat16 [2, 96, 768, 512], P('lev', 'lat', 'lon'), may hold values from -6 to 6
- cotangent: bfloat16 [2, 96, 768, 512], P('lev', 'lat', 'lon'), may hold values from -6 to 6
- land_mask: int32 [96, 768], P('lat', 'lon'), may hold values 0 or 1
- shift_offsets: int32 [2], replicated, may hold values from -40 to 39
- norm_gain: float32 [512], replicated, may hold values from 0.1 to 1.9
- w_qkv: bfloat16 [1536, 512], replicated, may hold values from -0.25 to 0.25
- w_proj: bfloat16 [512, 512], replicated, may hold values from -0.25 to 0.25
- rel_bias: float32 [8, 11, 23], replicated, may hold values from -260 to 260
Outputs:
- output: bfloat16 [2, 96, 768, 512], P('lev', 'lat', 'lon')
- grad_fields: bfloat16 [2, 96, 768, 512], P('lev', 'lat', 'lon')
- grad_qkv: float32 [1536, 512], P(('lon', 'lat', 'lev'))
- grad_proj: float32 [512, 512], P(('lon', 'lat', 'lev'))
- grad_bias: float32 [8, 11, 23], replicated
- grad_gain: float32 [512], replicated
All inputs are finite; a program needn't handle non-finite values. No bound on the sum of `land_mask` on one device may be relied on, other than what follows from the above.
Results may differ from a plain program's by a relative error of at most 0.009.
Values may be sent and summed in bfloat16 or wider, within the bound.
A program may use at most 128 MiB of HBM per device.

v0:
```python
import jax
import jax.numpy as jnp
from jax import lax
from jax.sharding import PartitionSpec as P

WROWS = 6
WCOLS = 12


EPSILON = 1e-05
NEG_FILL = 100.0


def extended_2(cells, sides, width, closed):
    for axis, dim in sides:
        count = lax.axis_size(axis)
        ends = count if closed else count - 1
        head = lax.slice_in_dim(cells, 0, width, axis=dim)
        tail = lax.slice_in_dim(cells, cells.shape[dim] - width, cells.shape[dim], axis=dim)
        cells = jnp.concatenate(
            [
                lax.ppermute(tail, axis, [(i, (i + 1) % count) for i in range(ends)]),
                cells,
                lax.ppermute(head, axis, [((i + 1) % count, i) for i in range(ends)]),
            ],
            axis=dim,
        )
    return cells


def offset_onehot():
    window_cells = WROWS * WCOLS
    cell_ids = jnp.arange(window_cells, dtype=jnp.int32)
    row_place = cell_ids // WCOLS
    col_place = cell_ids % WCOLS
    flat_offset = (row_place[:, None] - row_place[None, :] + WROWS - 1) * (2 * WCOLS - 1) + (
        col_place[:, None] - col_place[None, :] + WCOLS - 1
    )
    entries = (2 * WROWS - 1) * (2 * WCOLS - 1)
    return (jnp.arange(entries, dtype=jnp.int32)[:, None] == flat_offset.reshape(1, -1)).astype(
        jnp.float32
    )


def normalize(values, gain):
    widened = values.astype(jnp.float32)
    center = jnp.mean(widened, axis=-1, keepdims=True)
    spread = jnp.mean(jnp.square(widened - center), axis=-1, keepdims=True)
    inverse = lax.rsqrt(spread + EPSILON)
    scaled = (widened - center) * inverse
    return (scaled, inverse, (scaled * gain).astype(jnp.bfloat16))


def apply_linear(inputs, weight):
    return lax.dot_general(
        inputs, weight, (((inputs.ndim - 1,), (1,)), ((), ())), preferred_element_type=jnp.float32
    )


def to_windows(region, lat_count, lon_count):
    trailing = region.shape[2:]
    blocked = region.reshape((lat_count, WROWS, lon_count, WCOLS) + trailing)
    axes_order = (0, 2, 1, 3) + tuple(range(4, 4 + len(trailing)))
    return blocked.transpose(axes_order).reshape((lat_count * lon_count, WROWS * WCOLS) + trailing)


def from_windows(stacked, lat_count, lon_count):
    trailing = stacked.shape[2:]
    blocked = stacked.reshape((lat_count, lon_count, WROWS, WCOLS) + trailing)
    axes_order = (0, 2, 1, 3) + tuple(range(4, 4 + len(trailing)))
    return blocked.transpose(axes_order).reshape((lat_count * WROWS, lon_count * WCOLS) + trailing)


def extend(payload, grads_in, mask_half):
    taller = (
        extended_2(payload, (("lat", 0),), WROWS - 1, False),
        extended_2(grads_in, (("lat", 0),), WROWS - 1, False),
        extended_2(mask_half, (("lat", 0),), WROWS - 1, False),
    )
    return (
        extended_2(taller[0], (("lon", 1),), WCOLS - 1, True),
        extended_2(taller[1], (("lon", 1),), WCOLS - 1, True),
        extended_2(taller[2], (("lon", 1),), WCOLS - 1, True),
    )


def on_device(fields, cotangent, land_mask, shift_offsets, norm_gain, w_qkv, w_proj, rel_bias):
    own_tile = fields[0]
    grads_out = cotangent[0]
    row_count, col_count, model_width = own_tile.shape
    heads_count = rel_bias.shape[0]
    head_size = model_width // heads_count
    window_cells = WROWS * WCOLS
    lat_blocks = row_count // WROWS + 1
    region_rows = row_count + WROWS
    lat_shift = 1 + jnp.mod(shift_offsets[0], WROWS - 1)
    lon_shift = 1 + jnp.mod(shift_offsets[1], WCOLS - 1)
    zero_index = jnp.zeros((), jnp.int32)
    mask_half = land_mask.astype(jnp.bfloat16)
    lon_blocks = col_count // WCOLS + 1
    region_cols = col_count + WCOLS
    col_start = lon_shift - 1
    own_col = WCOLS - 1

    def region_of(extended):
        start_index = [lat_shift - 1, col_start] + [zero_index] * (extended.ndim - 2)
        return lax.dynamic_slice(
            extended, start_index, (region_rows, region_cols) + extended.shape[2:]
        )

    def own_part(extended):
        return extended[WROWS - 1 : WROWS - 1 + row_count, own_col : own_col + col_count]

    wide_fields, wide_grads, wide_mask = extend(own_tile, grads_out, mask_half)
    scaled_wide, inverse_wide, normed_wide = normalize(wide_fields, norm_gain)
    region_qkv = apply_linear(region_of(normed_wide), w_qkv).astype(jnp.bfloat16)
    scaled = own_part(scaled_wide)
    inverse = own_part(inverse_wide)
    normed = own_part(normed_wide)
    region_grads = region_of(wide_grads)
    region_mask = region_of(wide_mask)
    scaling = head_size ** (-0.5)
    onehot_table = offset_onehot()
    bias_full = jnp.dot(
        rel_bias.reshape(heads_count, -1), onehot_table, precision=lax.Precision.HIGHEST
    ).reshape(heads_count, window_cells, window_cells)
    stacked = to_windows(region_qkv, lat_blocks, lon_blocks).reshape(
        -1, window_cells, 3, heads_count, head_size
    )
    queries = stacked[:, :, 0]
    keys_w = stacked[:, :, 1]
    values_w = stacked[:, :, 2]
    key_mask = to_windows(region_mask, lat_blocks, lon_blocks).astype(jnp.float32)
    scores = (
        jnp.einsum("wihd,wjhd->whij", queries, keys_w, preferred_element_type=jnp.float32) * scaling
    )
    scores = scores + bias_full[None] + NEG_FILL * (key_mask[:, None, None, :] - 1.0)
    row_top = jnp.max(scores, axis=-1, keepdims=True)
    exp_scores = jnp.exp(scores - row_top)
    probs = exp_scores / jnp.sum(exp_scores, axis=-1, keepdims=True)
    probs_half = probs.astype(jnp.bfloat16)
    mixed = jnp.einsum(
        "whij,wjhd->wihd", probs_half, values_w, preferred_element_type=jnp.float32
    ).astype(jnp.bfloat16)
    mixed_region = from_windows(
        mixed.reshape(-1, window_cells, model_width), lat_blocks, lon_blocks
    )
    grads_windows = to_windows(region_grads, lat_blocks, lon_blocks).reshape(-1, model_width)
    grad_mixed = jnp.dot(grads_windows, w_proj, preferred_element_type=jnp.float32).astype(
        jnp.bfloat16
    )
    grad_mixed = grad_mixed.reshape(-1, window_cells, heads_count, head_size)
    grad_values = jnp.einsum(
        "whij,wihd->wjhd", probs_half, grad_mixed, preferred_element_type=jnp.float32
    )
    grad_probs = jnp.einsum(
        "wihd,wjhd->whij", grad_mixed, values_w, preferred_element_type=jnp.float32
    )
    grad_scores = probs * (grad_probs - jnp.sum(probs * grad_probs, axis=-1, keepdims=True))
    row_ids = jnp.arange(region_rows, dtype=jnp.int32)[:, None]
    col_ids = jnp.arange(region_cols, dtype=jnp.int32)[None, :]
    row_first = WROWS - lat_shift
    row_flag = (row_ids >= row_first) & (row_ids < row_first + row_count)
    col_first = WCOLS - lon_shift
    own_region = (row_flag & (col_ids >= col_first) & (col_ids < col_first + col_count)).astype(
        jnp.float32
    )
    own_flag = to_windows(own_region, lat_blocks, lon_blocks)
    bias_terms = jnp.sum(grad_scores * own_flag[:, None, :, None], axis=0).reshape(heads_count, -1)
    grad_table = jnp.dot(bias_terms, onehot_table.T, precision=lax.Precision.HIGHEST).reshape(
        rel_bias.shape
    )
    scores_half = grad_scores.astype(jnp.bfloat16)
    grad_queries = (
        jnp.einsum("whij,wjhd->wihd", scores_half, keys_w, preferred_element_type=jnp.float32)
        * scaling
    )
    grad_keys = (
        jnp.einsum("whij,wihd->wjhd", scores_half, queries, preferred_element_type=jnp.float32)
        * scaling
    )
    grad_cells = (
        jnp.stack([grad_queries, grad_keys, grad_values], axis=2)
        .astype(jnp.bfloat16)
        .reshape(-1, window_cells, 3 * model_width)
    )
    cells_region = from_windows(grad_cells, lat_blocks, lon_blocks)
    mixed_rows = lax.dynamic_slice_in_dim(mixed_region, row_first, row_count, 0)
    cells_rows = lax.dynamic_slice_in_dim(cells_region, row_first, row_count, 0)
    mixed_own = lax.dynamic_slice_in_dim(mixed_rows, WCOLS - lon_shift, col_count, 1)
    cells_own = lax.dynamic_slice_in_dim(cells_rows, WCOLS - lon_shift, col_count, 1)
    output = (own_tile.astype(jnp.float32) + apply_linear(mixed_own, w_proj)).astype(jnp.bfloat16)
    grad_cells_own = cells_own.reshape(-1, 3 * model_width)
    normed_flat = normed.reshape(-1, model_width)
    column_part = grad_cells_own
    grad_qkv_shard = lax.psum_scatter(
        lax.dot_general(
            column_part, normed_flat, (((0,), (0,)), ((), ())), preferred_element_type=jnp.float32
        ),
        ("lon", "lat", "lev"),
        scatter_dimension=0,
        tiled=True,
    )
    grad_normed = jnp.dot(grad_cells_own, w_qkv, preferred_element_type=jnp.float32)
    scaled_flat = scaled.reshape(-1, model_width)
    gain_term = jnp.sum(grad_normed * scaled_flat, axis=0)
    grad_scaled = grad_normed * norm_gain
    grad_input = inverse.reshape(-1, 1) * (
        grad_scaled
        - jnp.mean(grad_scaled, axis=-1, keepdims=True)
        - scaled_flat * jnp.mean(grad_scaled * scaled_flat, axis=-1, keepdims=True)
    )
    grads_flat = grads_out.reshape(-1, model_width)
    grad_fields = (
        (grads_flat.astype(jnp.float32) + grad_input)
        .astype(jnp.bfloat16)
        .reshape(1, row_count, col_count, model_width)
    )
    mixed_flat = mixed_own.reshape(-1, model_width)
    column_part = grads_flat
    grad_proj_shard = lax.psum_scatter(
        lax.dot_general(
            column_part, mixed_flat, (((0,), (0,)), ((), ())), preferred_element_type=jnp.float32
        ),
        ("lon", "lat", "lev"),
        scatter_dimension=0,
        tiled=True,
    )
    grad_bias, grad_gain = lax.psum((grad_table, gain_term), ("lon", "lat", "lev"))
    return (
        output.reshape(1, row_count, col_count, model_width),
        grad_fields,
        grad_qkv_shard,
        grad_proj_shard,
        grad_bias,
        grad_gain,
    )


def solution(mesh):
    return jax.shard_map(
        on_device,
        mesh=mesh,
        in_specs=(
            P("lev", "lat", "lon", None),
            P("lev", "lat", "lon", None),
            P("lat", "lon"),
            P(),
            P(),
            P(),
            P(),
            P(),
        ),
        out_specs=(
            P("lev", "lat", "lon", None),
            P("lev", "lat", "lon", None),
            P(("lon", "lat", "lev"), None),
            P(("lon", "lat", "lev"), None),
            P(),
            P(),
        ),
        check_vma=False,
    )
```

profile of v0, /device:TPU:24, one launch (start us, length us, event | category | flops | bytes accessed | tf_op | source)
XLA Modules:
  0.0 1589.9 jit_solution(2501697353240296294)
XLA Ops:
  8.6 4.6 collective-permute-start.4
  13.2 12.6 collective-permute-start.5
  27.7 4.8 collective-permute-start
  37.7 10.6 collective-permute-start.9
  56.8 13.6 collective-permute-start.1
  73.1 11.8 collective-permute-start.11
  84.9 11.8 collective-permute-start.10
  96.8 11.8 collective-permute-start.6
  108.7 11.8 collective-permute-start.7
  121.5 11.8 collective-permute-start.2
  133.3 12.3 collective-permute-start.3
  175.6 5.7 reshape.262
  181.3 4.8 copy.115
  186.2 9.9 reshape_reshape.10
  196.0 5.8 fusion.52
  209.1 4.4 copy.113
  231.5 9.6 copy.99
  241.1 10.0 convert_element_type.77
  251.2 4.7 copy.100
  255.9 6.1 reshape.268
  265.3 4.2 convolution_bitcast_fusion.1
  269.5 656.8 %fusion = f32[8,512]{1,0:T(8,128)S(1)} fusion(f32[1536,512]{1,0:T(8,128)} %convolution_bitcast_fusion.1), kind=kCustom, calls=%all-reduce-scatter | all-reduce-scatter fusion | flops 1048577 | bytes 3162112
  927.6 15.3 collective-permute-start.73
  942.9 7.1 collective-permute-start.72
  955.3 4.3 collective-permute-start.70
  975.9 10.5 collective-permute-start.58
  994.0 4.6 collective-permute-start.55
  1005.7 4.3 convert_bitcast_fusion.1
  1039.7 6.3 collective-permute-start.43
  1046.0 13.1 collective-permute-start.42
  1063.4 13.1 collective-permute-start.41
  1076.6 13.1 collective-permute-start.40
  1089.7 13.1 collective-permute-start.39
  1102.9 13.1 collective-permute-start.38
  1116.0 13.1 collective-permute-start.37
  1129.2 4.9 multiply_reduce_fusion.4
  1134.1 13.2 collective-permute-start.36
  1147.3 13.1 collective-permute-start.35
  1160.5 13.1 collective-permute-start.34
  1173.6 13.1 collective-permute-start.33
  1186.8 13.1 collective-permute-start.32
  1199.9 13.1 collective-permute-start.31
  1213.1 13.1 collective-permute-start.30
  1226.2 13.1 collective-permute-start.29
  1239.4 13.1 collective-permute-start.28
  1252.5 13.1 collective-permute-start.27
  1265.9 13.7 collective-permute-start.26
  1279.6 13.1 collective-permute-start.25
  1292.8 13.1 collective-permute-start.24
  1305.9 13.2 collective-permute-start.23
  1319.1 13.1 collective-permute-start.22
  1335.8 12.7 collective-permute-start.21
  1348.5 13.1 collective-permute-start.20
  1361.6 13.1 collective-permute-start.19
  1374.8 13.1 collective-permute-start.18
  1387.9 13.4 collective-permute-start.17
  1401.3 7.4 fusion.2
  1408.7 13.1 collective-permute-start.16
  1421.9 13.1 collective-permute-start.15
  1435.0 13.1 collective-permute-start.14
  1448.2 13.1 collective-permute-start.13
  1461.3 13.1 collective-permute-start.12
  1476.9 78.4 %all-reduce.3 = (f32[8,11,23]{2,0,1:T(8,128)}, f32[512]{0:T(512)}) all-reduce(f32[8,11,23]{2,0,1:T(8,128)S(1)} %fusion.2, f32[512]{0:T(512)S(1)} %copy-done.102), channel_id=1, replica_groups=mesh['lon'=16,'lat'=8,'lev'=2] {'lon','lat','lev'}, use_global_device_ids=true, to_apply=%region_10.11 | all-reduce | flops 2536 | bytes 20288 | tf_op jit(solution)/shard_map/psum | solution.py:229
  1555.6 24.8 %concatenate.24 = f32[518,512]{1,0:T(8,128)S(1)} concatenate(f32[6,512]{1,0:T(8,128)S(1)} %copy-done.31, f32[8,512]{1,0:T(8,128)S(1)} %copy-done.25, f32[8,512]{1,0:T(8,128)S(1)} %copy-done.27, f32[8,512]{1,0:T(8,128)S(1)} %copy-done.29, f32[8,512]{1,0:T(8,128)S(1)} %copy-done.33, f32[8,512]{1,0:T(8,128)S(1)} %copy-done.35, f32[8,512]{1,0:T(8,128)S(1)} %copy-done.37, ...), dimensions={0} | concatenate | bytes 2121728
  (382 shorter events, 156.8 us)
Async XLA Ops:
  7.2 1573.9 %all-reduce.6.cloned.1.call-start = ((), (), s32[]{:S(2)}) async-start(), calls=%async_computation | async-start | bytes 2097152
  8.6 48.1 %collective-permute-start.4 = (bf16[5,48]{1,0:T(8,128)(2,1)}, bf16[5,48]{1,0:T(8,128)(2,1)S(1)}, u32[]{:S(2)}, u32[]{:S(2)}) collective-permute-start(bf16[5,48]{1,0:T(8,128)(2,1)} %get-tuple-element.62), channel_id=1, source_target_pairs={{0,2},{2,4},{4,6},{6,8},{8,10},{10,12},{12,14},{1,3},{3,5},{5,7},{... | collective-permute-start | bytes 1448 | tf_op jit(solution)/shard_map/ppermute | solution.py:22
  13.2 57.1 %collective-permute-start.5 = (bf16[5,48]{1,0:T(8,128)(2,1)}, bf16[5,48]{1,0:T(8,128)(2,1)}, u32[]{:S(2)}, u32[]{:S(2)}) collective-permute-start(bf16[5,48]{1,0:T(8,128)(2,1)} %get-tuple-element.63), channel_id=1, source_target_pairs={{2,0},{4,2},{6,4},{8,6},{10,8},{12,10},{14,12},{3,1},{5,3},{7,5},{... | collective-permute-start | bytes 1448 | tf_op jit(solution)/shard_map/ppermute | solution.py:24
  27.7 81.0 %collective-permute-start = (bf16[5,48,512]{2,1,0:T(8,128)(2,1)}, bf16[5,48,512]{2,1,0:T(8,128)(2,1)S(1)}, u32[]{:S(2)}, u32[]{:S(2)}) collective-permute-start(bf16[5,48,512]{2,1,0:T(8,128)(2,1)} %get-tuple-element.56), channel_id=1, source_target_pairs={{0,2},{2,4},{4,6},{6,8},{8,10},{10,12},{12,14},{1,3},{3,5},{5,7},{... | collective-permute-start | bytes 737288 | tf_op jit(solution)/shard_map/ppermute | solution.py:22
  34.4 36.7 %collective-permute-start.8 = (bf16[5,48,512]{2,1,0:T(8,128)(2,1)}, bf16[5,48,512]{2,1,0:T(8,128)(2,1)S(1)}, u32[]{:S(2)}, u32[]{:S(2)}) collective-permute-start(bf16[5,48,512]{2,1,0:T(8,128)(2,1)} %get-tuple-element.54), channel_id=1, source_target_pairs={{0,2},{2,4},{4,6},{6,8},{8,10},{10,12},{12,14},{1,3},{3,5},{5,7},{... | collective-permute-start | bytes 737288 | tf_op jit(solution)/shard_map/ppermute | solution.py:22
  37.7 33.3 %collective-permute-start.9 = (bf16[5,48,512]{2,1,0:T(8,128)(2,1)}, bf16[5,48,512]{2,1,0:T(8,128)(2,1)}, u32[]{:S(2)}, u32[]{:S(2)}) collective-permute-start(bf16[5,48,512]{2,1,0:T(8,128)(2,1)} %get-tuple-element.55), channel_id=1, source_target_pairs={{2,0},{4,2},{6,4},{8,6},{10,8},{12,10},{14,12},{3,1},{5,3},{7,5},{... | collective-permute-start | bytes 737288 | tf_op jit(solution)/shard_map/ppermute | solution.py:24
  56.8 63.7 %collective-permute-start.1 = (bf16[5,48,512]{2,1,0:T(8,128)(2,1)}, bf16[5,48,512]{2,1,0:T(8,128)(2,1)S(1)}, u32[]{:S(2)}, u32[]{:S(2)}) collective-permute-start(bf16[5,48,512]{2,1,0:T(8,128)(2,1)} %get-tuple-element.57), channel_id=1, source_target_pairs={{2,0},{4,2},{6,4},{8,6},{10,8},{12,10},{14,12},{3,1},{5,3},{7,5},{... | collective-permute-start | bytes 737288 | tf_op jit(solution)/shard_map/ppermute | solution.py:24
  73.1 74.2 %collective-permute-start.11 = (bf16[22,11,512]{2,1,0:T(8,128)(2,1)}, bf16[22,11,512]{2,1,0:T(8,128)(2,1)}, u32[]{:S(2)}, u32[]{:S(2)}) collective-permute-start(bf16[22,11,512]{2,1,0:T(8,128)(2,1)} %get-tuple-element.50), channel_id=1, source_target_pairs={{16,0},{32,16},{48,32},{64,48},{80,64},{96,80},{112,96},{128,112},... | collective-permute-start | bytes 743432 | tf_op jit(solution)/shard_map/ppermute | solution.py:24
  84.9 62.4 %collective-permute-start.10 = (bf16[22,11,512]{2,1,0:T(8,128)(2,1)}, bf16[22,11,512]{2,1,0:T(8,128)(2,1)}, u32[]{:S(2)}, u32[]{:S(2)}) collective-permute-start(bf16[22,11,512]{2,1,0:T(8,128)(2,1)} %get-tuple-element.51), channel_id=1, source_target_pairs={{0,16},{16,32},{32,48},{48,64},{64,80},{80,96},{96,112},{112,128},... | collective-permute-start | bytes 743432 | tf_op jit(solution)/shard_map/ppermute | solution.py:22
  96.8 36.5 %collective-permute-start.6 = (bf16[22,11]{1,0:T(8,128)(2,1)S(1)}, bf16[22,11]{1,0:T(8,128)(2,1)S(1)}, u32[]{:S(2)}, u32[]{:S(2)}) collective-permute-start(bf16[22,11]{1,0:T(8,128)(2,1)S(1)} %get-tuple-element.60), channel_id=1, source_target_pairs={{0,16},{16,32},{32,48},{48,64},{64,80},{80,96},{96,112},{112,128},... | collective-permute-start | bytes 1460 | tf_op jit(solution)/shard_map/ppermute | solution.py:22
  108.7 37.0 %collective-permute-start.7 = (bf16[22,11]{1,0:T(8,128)(2,1)S(1)}, bf16[22,11]{1,0:T(8,128)(2,1)S(1)}, u32[]{:S(2)}, u32[]{:S(2)}) collective-permute-start(bf16[22,11]{1,0:T(8,128)(2,1)S(1)} %get-tuple-element.61), channel_id=1, source_target_pairs={{16,0},{32,16},{48,32},{64,48},{80,64},{96,80},{112,96},{128,112},... | collective-permute-start | bytes 1460 | tf_op jit(solution)/shard_map/ppermute | solution.py:24
  121.5 33.1 %collective-permute-start.2 = (bf16[22,11,512]{2,1,0:T(8,128)(2,1)}, bf16[22,11,512]{2,1,0:T(8,128)(2,1)}, u32[]{:S(2)}, u32[]{:S(2)}) collective-permute-start(bf16[22,11,512]{2,1,0:T(8,128)(2,1)} %get-tuple-element.52), channel_id=1, source_target_pairs={{0,16},{16,32},{32,48},{48,64},{64,80},{80,96},{96,112},{112,128},... | collective-permute-start | bytes 743432 | tf_op jit(solution)/shard_map/ppermute | solution.py:22
  133.3 21.2 %collective-permute-start.3 = (bf16[22,11,512]{2,1,0:T(8,128)(2,1)}, bf16[22,11,512]{2,1,0:T(8,128)(2,1)}, u32[]{:S(2)}, u32[]{:S(2)}) collective-permute-start(bf16[22,11,512]{2,1,0:T(8,128)(2,1)} %get-tuple-element.53), channel_id=1, source_target_pairs={{16,0},{32,16},{48,32},{64,48},{80,64},{96,80},{112,96},{128,112},... | collective-permute-start | bytes 743432 | tf_op jit(solution)/shard_map/ppermute | solution.py:24
  926.3 33.3 %collective-permute-start.74 = (f32[8,512]{1,0:T(8,128)S(1)}, f32[8,512]{1,0:T(8,128)S(1)}, u32[]{:S(2)}, u32[]{:S(2)}) collective-permute-start(f32[8,512]{1,0:T(8,128)S(1)} %fusion), channel_id=1, source_target_pairs={{0,63},{1,64},{2,65},{3,66},{4,67},{5,68},{6,69},{7,70},{8,71},{9,... | collective-permute-start | bytes 49160
  927.6 33.3 %collective-permute-start.73 = (f32[8,512]{1,0:T(8,128)S(1)}, f32[8,512]{1,0:T(8,128)S(1)}, u32[]{:S(2)}, u32[]{:S(2)}) collective-permute-start(f32[8,512]{1,0:T(8,128)S(1)} %fusion), channel_id=1, source_target_pairs={{0,62},{1,63},{2,64},{3,65},{4,66},{5,67},{6,68},{7,69},{8,70},{9,... | collective-permute-start | bytes 49160
  942.9 19.3 %collective-permute-start.72 = (f32[8,512]{1,0:T(8,128)S(1)}, f32[8,512]{1,0:T(8,128)S(1)}, u32[]{:S(2)}, u32[]{:S(2)}) collective-permute-start(f32[8,512]{1,0:T(8,128)S(1)} %fusion), channel_id=1, source_target_pairs={{0,61},{1,62},{2,63},{3,64},{4,65},{5,66},{6,67},{7,68},{8,69},{9,... | collective-permute-start | bytes 49160
  968.9 17.5 %collective-permute-start.62 = (f32[8,512]{1,0:T(8,128)S(1)}, f32[8,512]{1,0:T(8,128)S(1)}, u32[]{:S(2)}, u32[]{:S(2)}) collective-permute-start(f32[8,512]{1,0:T(8,128)S(1)} %fusion), channel_id=1, source_target_pairs={{0,51},{1,52},{2,53},{3,54},{4,55},{5,56},{6,57},{7,58},{8,59},{9,... | collective-permute-start | bytes 49160
  970.2 19.8 %collective-permute-start.61 = (f32[8,512]{1,0:T(8,128)S(1)}, f32[8,512]{1,0:T(8,128)}, u32[]{:S(2)}, u32[]{:S(2)}) collective-permute-start(f32[8,512]{1,0:T(8,128)S(1)} %fusion), channel_id=1, source_target_pairs={{0,50},{1,51},{2,52},{3,53},{4,54},{5,55},{6,56},{7,57},{8,58},{9,... | collective-permute-start | bytes 49160
  972.1 21.9 %collective-permute-start.60 = (f32[8,512]{1,0:T(8,128)S(1)}, f32[8,512]{1,0:T(8,128)}, u32[]{:S(2)}, u32[]{:S(2)}) collective-permute-start(f32[8,512]{1,0:T(8,128)S(1)} %fusion), channel_id=1, source_target_pairs={{0,49},{1,50},{2,51},{3,52},{4,53},{5,54},{6,55},{7,56},{8,57},{9,... | collective-permute-start | bytes 49160
  974.0 24.6 %collective-permute-start.59 = (f32[8,512]{1,0:T(8,128)S(1)}, f32[8,512]{1,0:T(8,128)}, u32[]{:S(2)}, u32[]{:S(2)}) collective-permute-start(f32[8,512]{1,0:T(8,128)S(1)} %fusion), channel_id=1, source_target_pairs={{0,48},{1,49},{2,50},{3,51},{4,52},{5,53},{6,54},{7,55},{8,56},{9,... | collective-permute-start | bytes 49160
  975.9 24.9 %collective-permute-start.58 = (f32[8,512]{1,0:T(8,128)S(1)}, f32[8,512]{1,0:T(8,128)}, u32[]{:S(2)}, u32[]{:S(2)}) collective-permute-start(f32[8,512]{1,0:T(8,128)S(1)} %fusion), channel_id=1, source_target_pairs={{0,47},{1,48},{2,49},{3,50},{4,51},{5,52},{6,53},{7,54},{8,55},{9,... | collective-permute-start | bytes 49160
  987.1 16.8 %collective-permute-start.57 = (f32[8,512]{1,0:T(8,128)S(1)}, f32[8,512]{1,0:T(8,128)}, u32[]{:S(2)}, u32[]{:S(2)}) collective-permute-start(f32[8,512]{1,0:T(8,128)S(1)} %fusion), channel_id=1, source_target_pairs={{0,46},{1,47},{2,48},{3,49},{4,50},{5,51},{6,52},{7,53},{8,54},{9,... | collective-permute-start | bytes 49160
  989.9 32.0 %collective-permute-start.56 = (f32[8,512]{1,0:T(8,128)S(1)}, f32[8,512]{1,0:T(8,128)}, u32[]{:S(2)}, u32[]{:S(2)}) collective-permute-start(f32[8,512]{1,0:T(8,128)S(1)} %fusion), channel_id=1, source_target_pairs={{0,45},{1,46},{2,47},{3,48},{4,49},{5,50},{6,51},{7,52},{8,53},{9,... | collective-permute-start | bytes 49160
  994.0 29.3 %collective-permute-start.55 = (f32[8,512]{1,0:T(8,128)S(1)}, f32[8,512]{1,0:T(8,128)}, u32[]{:S(2)}, u32[]{:S(2)}) collective-permute-start(f32[8,512]{1,0:T(8,128)S(1)} %fusion), channel_id=1, source_target_pairs={{0,44},{1,45},{2,46},{3,47},{4,48},{5,49},{6,50},{7,51},{8,52},{9,... | collective-permute-start | bytes 49160
  998.6 28.1 %collective-permute-start.54 = (f32[8,512]{1,0:T(8,128)S(1)}, f32[8,512]{1,0:T(8,128)}, u32[]{:S(2)}, u32[]{:S(2)}) collective-permute-start(f32[8,512]{1,0:T(8,128)S(1)} %fusion), channel_id=1, source_target_pairs={{0,43},{1,44},{2,45},{3,46},{4,47},{5,48},{6,49},{7,50},{8,51},{9,... | collective-permute-start | bytes 49160
  1000.7 27.6 %collective-permute-start.53 = (f32[8,512]{1,0:T(8,128)S(1)}, f32[8,512]{1,0:T(8,128)}, u32[]{:S(2)}, u32[]{:S(2)}) collective-permute-start(f32[8,512]{1,0:T(8,128)S(1)} %fusion), channel_id=1, source_target_pairs={{0,42},{1,43},{2,44},{3,45},{4,46},{5,47},{6,48},{7,49},{8,50},{9,... | collective-permute-start | bytes 49160
  1003.9 27.6 %collective-permute-start.52 = (f32[8,512]{1,0:T(8,128)S(1)}, f32[8,512]{1,0:T(8,128)}, u32[]{:S(2)}, u32[]{:S(2)}) collective-permute-start(f32[8,512]{1,0:T(8,128)S(1)} %fusion), channel_id=1, source_target_pairs={{0,41},{1,42},{2,43},{3,44},{4,45},{5,46},{6,47},{7,48},{8,49},{9,... | collective-permute-start | bytes 49160
  1021.9 13.5 collective-permute-start.51
  1031.5 14.5 collective-permute-start.47
  1035.5 27.9 %collective-permute-start.46 = (f32[8,512]{1,0:T(8,128)S(1)}, f32[8,512]{1,0:T(8,128)S(1)}, u32[]{:S(2)}, u32[]{:S(2)}) collective-permute-start(f32[8,512]{1,0:T(8,128)S(1)} %fusion), channel_id=1, source_target_pairs={{0,35},{1,36},{2,37},{3,38},{4,39},{5,40},{6,41},{7,42},{8,43},{9,... | collective-permute-start | bytes 49160
  1036.8 39.7 %collective-permute-start.45 = (f32[8,512]{1,0:T(8,128)S(1)}, f32[8,512]{1,0:T(8,128)S(1)}, u32[]{:S(2)}, u32[]{:S(2)}) collective-permute-start(f32[8,512]{1,0:T(8,128)S(1)} %fusion), channel_id=1, source_target_pairs={{0,34},{1,35},{2,36},{3,37},{4,38},{5,39},{6,40},{7,41},{8,42},{9,... | collective-permute-start | bytes 49160
  1038.4 51.3 %collective-permute-start.44 = (f32[8,512]{1,0:T(8,128)S(1)}, f32[8,512]{1,0:T(8,128)S(1)}, u32[]{:S(2)}, u32[]{:S(2)}) collective-permute-start(f32[8,512]{1,0:T(8,128)S(1)} %fusion), channel_id=1, source_target_pairs={{0,33},{1,34},{2,35},{3,36},{4,37},{5,38},{6,39},{7,40},{8,41},{9,... | collective-permute-start | bytes 49160
  1039.7 63.2 %collective-permute-start.43 = (f32[8,512]{1,0:T(8,128)S(1)}, f32[8,512]{1,0:T(8,128)S(1)}, u32[]{:S(2)}, u32[]{:S(2)}) collective-permute-start(f32[8,512]{1,0:T(8,128)S(1)} %fusion), channel_id=1, source_target_pairs={{0,32},{1,33},{2,34},{3,35},{4,36},{5,37},{6,38},{7,39},{8,40},{9,... | collective-permute-start | bytes 49160
  1046.0 70.0 %collective-permute-start.42 = (f32[8,512]{1,0:T(8,128)S(1)}, f32[8,512]{1,0:T(8,128)S(1)}, u32[]{:S(2)}, u32[]{:S(2)}) collective-permute-start(f32[8,512]{1,0:T(8,128)S(1)} %fusion), channel_id=1, source_target_pairs={{0,31},{1,32},{2,33},{3,34},{4,35},{5,36},{6,37},{7,38},{8,39},{9,... | collective-permute-start | bytes 49160
  1063.4 70.7 %collective-permute-start.41 = (f32[8,512]{1,0:T(8,128)S(1)}, f32[8,512]{1,0:T(8,128)S(1)}, u32[]{:S(2)}, u32[]{:S(2)}) collective-permute-start(f32[8,512]{1,0:T(8,128)S(1)} %fusion), channel_id=1, source_target_pairs={{0,30},{1,31},{2,32},{3,33},{4,34},{5,35},{6,36},{7,37},{8,38},{9,... | collective-permute-start | bytes 49160
  1076.6 70.8 %collective-permute-start.40 = (f32[8,512]{1,0:T(8,128)S(1)}, f32[8,512]{1,0:T(8,128)S(1)}, u32[]{:S(2)}, u32[]{:S(2)}) collective-permute-start(f32[8,512]{1,0:T(8,128)S(1)} %fusion), channel_id=1, source_target_pairs={{0,29},{1,30},{2,31},{3,32},{4,33},{5,34},{6,35},{7,36},{8,37},{9,... | collective-permute-start | bytes 49160
  1089.7 70.8 %collective-permute-start.39 = (f32[8,512]{1,0:T(8,128)S(1)}, f32[8,512]{1,0:T(8,128)S(1)}, u32[]{:S(2)}, u32[]{:S(2)}) collective-permute-start(f32[8,512]{1,0:T(8,128)S(1)} %fusion), channel_id=1, source_target_pairs={{0,28},{1,29},{2,30},{3,31},{4,32},{5,33},{6,34},{7,35},{8,36},{9,... | collective-permute-start | bytes 49160
  1102.9 70.8 %collective-permute-start.38 = (f32[8,512]{1,0:T(8,128)S(1)}, f32[8,512]{1,0:T(8,128)S(1)}, u32[]{:S(2)}, u32[]{:S(2)}) collective-permute-start(f32[8,512]{1,0:T(8,128)S(1)} %fusion), channel_id=1, source_target_pairs={{0,27},{1,28},{2,29},{3,30},{4,31},{5,32},{6,33},{7,34},{8,35},{9,... | collective-permute-start | bytes 49160
  1116.0 70.8 %collective-permute-start.37 = (f32[8,512]{1,0:T(8,128)S(1)}, f32[8,512]{1,0:T(8,128)S(1)}, u32[]{:S(2)}, u32[]{:S(2)}) collective-permute-start(f32[8,512]{1,0:T(8,128)S(1)} %fusion), channel_id=1, source_target_pairs={{0,26},{1,27},{2,28},{3,29},{4,30},{5,31},{6,32},{7,33},{8,34},{9,... | collective-permute-start | bytes 49160
  1134.1 65.9 %collective-permute-start.36 = (f32[8,512]{1,0:T(8,128)S(1)}, f32[8,512]{1,0:T(8,128)S(1)}, u32[]{:S(2)}, u32[]{:S(2)}) collective-permute-start(f32[8,512]{1,0:T(8,128)S(1)} %fusion), channel_id=1, source_target_pairs={{0,25},{1,26},{2,27},{3,28},{4,29},{5,30},{6,31},{7,32},{8,33},{9,... | collective-permute-start | bytes 49160
  1147.3 65.7 %collective-permute-start.35 = (f32[8,512]{1,0:T(8,128)S(1)}, f32[8,512]{1,0:T(8,128)S(1)}, u32[]{:S(2)}, u32[]{:S(2)}) collective-permute-start(f32[8,512]{1,0:T(8,128)S(1)} %fusion), channel_id=1, source_target_pairs={{0,24},{1,25},{2,26},{3,27},{4,28},{5,29},{6,30},{7,31},{8,32},{9,... | collective-permute-start | bytes 49160
  1160.5 65.7 %collective-permute-start.34 = (f32[8,512]{1,0:T(8,128)S(1)}, f32[8,512]{1,0:T(8,128)S(1)}, u32[]{:S(2)}, u32[]{:S(2)}) collective-permute-start(f32[8,512]{1,0:T(8,128)S(1)} %fusion), channel_id=1, source_target_pairs={{0,23},{1,24},{2,25},{3,26},{4,27},{5,28},{6,29},{7,30},{8,31},{9,... | collective-permute-start | bytes 49160
  1173.6 65.7 %collective-permute-start.33 = (f32[8,512]{1,0:T(8,128)S(1)}, f32[8,512]{1,0:T(8,128)S(1)}, u32[]{:S(2)}, u32[]{:S(2)}) collective-permute-start(f32[8,512]{1,0:T(8,128)S(1)} %fusion), channel_id=1, source_target_pairs={{0,22},{1,23},{2,24},{3,25},{4,26},{5,27},{6,28},{7,29},{8,30},{9,... | collective-permute-start | bytes 49160
  1186.8 65.7 %collective-permute-start.32 = (f32[8,512]{1,0:T(8,128)S(1)}, f32[8,512]{1,0:T(8,128)S(1)}, u32[]{:S(2)}, u32[]{:S(2)}) collective-permute-start(f32[8,512]{1,0:T(8,128)S(1)} %fusion), channel_id=1, source_target_pairs={{0,21},{1,22},{2,23},{3,24},{4,25},{5,26},{6,27},{7,28},{8,29},{9,... | collective-permute-start | bytes 49160
  1199.9 65.9 %collective-permute-start.31 = (f32[8,512]{1,0:T(8,128)S(1)}, f32[8,512]{1,0:T(8,128)S(1)}, u32[]{:S(2)}, u32[]{:S(2)}) collective-permute-start(f32[8,512]{1,0:T(8,128)S(1)} %fusion), channel_id=1, source_target_pairs={{0,20},{1,21},{2,22},{3,23},{4,24},{5,25},{6,26},{7,27},{8,28},{9,... | collective-permute-start | bytes 49160
  1213.1 66.5 %collective-permute-start.30 = (f32[8,512]{1,0:T(8,128)S(1)}, f32[8,512]{1,0:T(8,128)S(1)}, u32[]{:S(2)}, u32[]{:S(2)}) collective-permute-start(f32[8,512]{1,0:T(8,128)S(1)} %fusion), channel_id=1, source_target_pairs={{0,19},{1,20},{2,21},{3,22},{4,23},{5,24},{6,25},{7,26},{8,27},{9,... | collective-permute-start | bytes 49160
  1226.2 66.5 %collective-permute-start.29 = (f32[8,512]{1,0:T(8,128)S(1)}, f32[8,512]{1,0:T(8,128)S(1)}, u32[]{:S(2)}, u32[]{:S(2)}) collective-permute-start(f32[8,512]{1,0:T(8,128)S(1)} %fusion), channel_id=1, source_target_pairs={{0,18},{1,19},{2,20},{3,21},{4,22},{5,23},{6,24},{7,25},{8,26},{9,... | collective-permute-start | bytes 49160
  1239.4 66.5 %collective-permute-start.28 = (f32[8,512]{1,0:T(8,128)S(1)}, f32[8,512]{1,0:T(8,128)S(1)}, u32[]{:S(2)}, u32[]{:S(2)}) collective-permute-start(f32[8,512]{1,0:T(8,128)S(1)} %fusion), channel_id=1, source_target_pairs={{0,17},{1,18},{2,19},{3,20},{4,21},{5,22},{6,23},{7,24},{8,25},{9,... | collective-permute-start | bytes 49160
  1252.5 66.5 %collective-permute-start.27 = (f32[8,512]{1,0:T(8,128)S(1)}, f32[8,512]{1,0:T(8,128)S(1)}, u32[]{:S(2)}, u32[]{:S(2)}) collective-permute-start(f32[8,512]{1,0:T(8,128)S(1)} %fusion), channel_id=1, source_target_pairs={{0,16},{1,17},{2,18},{3,19},{4,20},{5,21},{6,22},{7,23},{8,24},{9,... | collective-permute-start | bytes 49160
  1265.9 69.9 %collective-permute-start.26 = (f32[8,512]{1,0:T(8,128)S(1)}, f32[8,512]{1,0:T(8,128)}, u32[]{:S(2)}, u32[]{:S(2)}) collective-permute-start(f32[8,512]{1,0:T(8,128)S(1)} %fusion), channel_id=1, source_target_pairs={{0,15},{1,16},{2,17},{3,18},{4,19},{5,20},{6,21},{7,22},{8,23},{9,... | collective-permute-start | bytes 49160
  1279.6 68.9 %collective-permute-start.25 = (f32[8,512]{1,0:T(8,128)S(1)}, f32[8,512]{1,0:T(8,128)}, u32[]{:S(2)}, u32[]{:S(2)}) collective-permute-start(f32[8,512]{1,0:T(8,128)S(1)} %fusion), channel_id=1, source_target_pairs={{0,14},{1,15},{2,16},{3,17},{4,18},{5,19},{6,20},{7,21},{8,22},{9,... | collective-permute-start | bytes 49160
  1292.8 68.9 %collective-permute-start.24 = (f32[8,512]{1,0:T(8,128)S(1)}, f32[8,512]{1,0:T(8,128)}, u32[]{:S(2)}, u32[]{:S(2)}) collective-permute-start(f32[8,512]{1,0:T(8,128)S(1)} %fusion), channel_id=1, source_target_pairs={{0,13},{1,14},{2,15},{3,16},{4,17},{5,18},{6,19},{7,20},{8,21},{9,... | collective-permute-start | bytes 49160
  1305.9 68.8 %collective-permute-start.23 = (f32[8,512]{1,0:T(8,128)S(1)}, f32[8,512]{1,0:T(8,128)}, u32[]{:S(2)}, u32[]{:S(2)}) collective-permute-start(f32[8,512]{1,0:T(8,128)S(1)} %fusion), channel_id=1, source_target_pairs={{0,12},{1,13},{2,14},{3,15},{4,16},{5,17},{6,18},{7,19},{8,20},{9,... | collective-permute-start | bytes 49160
  1319.1 68.8 %collective-permute-start.22 = (f32[8,512]{1,0:T(8,128)S(1)}, f32[8,512]{1,0:T(8,128)}, u32[]{:S(2)}, u32[]{:S(2)}) collective-permute-start(f32[8,512]{1,0:T(8,128)S(1)} %fusion), channel_id=1, source_target_pairs={{0,11},{1,12},{2,13},{3,14},{4,15},{5,16},{6,17},{7,18},{8,19},{9,... | collective-permute-start | bytes 49160
  1335.8 72.9 %collective-permute-start.21 = (f32[8,512]{1,0:T(8,128)S(1)}, f32[8,512]{1,0:T(8,128)S(1)}, u32[]{:S(2)}, u32[]{:S(2)}) collective-permute-start(f32[8,512]{1,0:T(8,128)S(1)} %fusion), channel_id=1, source_target_pairs={{0,10},{1,11},{2,12},{3,13},{4,14},{5,15},{6,16},{7,17},{8,18},{9,... | collective-permute-start | bytes 49160
  1348.5 73.4 %collective-permute-start.20 = (f32[8,512]{1,0:T(8,128)S(1)}, f32[8,512]{1,0:T(8,128)S(1)}, u32[]{:S(2)}, u32[]{:S(2)}) collective-permute-start(f32[8,512]{1,0:T(8,128)S(1)} %fusion), channel_id=1, source_target_pairs={{0,9},{1,10},{2,11},{3,12},{4,13},{5,14},{6,15},{7,16},{8,17},{9,1... | collective-permute-start | bytes 49160
  1361.6 73.4 %collective-permute-start.19 = (f32[8,512]{1,0:T(8,128)S(1)}, f32[8,512]{1,0:T(8,128)S(1)}, u32[]{:S(2)}, u32[]{:S(2)}) collective-permute-start(f32[8,512]{1,0:T(8,128)S(1)} %fusion), channel_id=1, source_target_pairs={{0,8},{1,9},{2,10},{3,11},{4,12},{5,13},{6,14},{7,15},{8,16},{9,17... | collective-permute-start | bytes 49160
  1374.8 73.4 %collective-permute-start.18 = (f32[8,512]{1,0:T(8,128)S(1)}, f32[8,512]{1,0:T(8,128)S(1)}, u32[]{:S(2)}, u32[]{:S(2)}) collective-permute-start(f32[8,512]{1,0:T(8,128)S(1)} %fusion), channel_id=1, source_target_pairs={{0,7},{1,8},{2,9},{3,10},{4,11},{5,12},{6,13},{7,14},{8,15},{9,16}... | collective-permute-start | bytes 49160
  1387.9 73.4 %collective-permute-start.17 = (f32[8,512]{1,0:T(8,128)S(1)}, f32[8,512]{1,0:T(8,128)S(1)}, u32[]{:S(2)}, u32[]{:S(2)}) collective-permute-start(f32[8,512]{1,0:T(8,128)S(1)} %fusion), channel_id=1, source_target_pairs={{0,6},{1,7},{2,8},{3,9},{4,10},{5,11},{6,12},{7,13},{8,14},{9,15},... | collective-permute-start | bytes 49160
  1408.7 146.6 %collective-permute-start.16 = (f32[8,512]{1,0:T(8,128)S(1)}, f32[8,512]{1,0:T(8,128)S(1)}, u32[]{:S(2)}, u32[]{:S(2)}) collective-permute-start(f32[8,512]{1,0:T(8,128)S(1)} %fusion), channel_id=1, source_target_pairs={{0,5},{1,6},{2,7},{3,8},{4,9},{5,10},{6,11},{7,12},{8,13},{9,14},{... | collective-permute-start | bytes 49160
  1421.9 133.4 %collective-permute-start.15 = (f32[8,512]{1,0:T(8,128)S(1)}, f32[8,512]{1,0:T(8,128)S(1)}, u32[]{:S(2)}, u32[]{:S(2)}) collective-permute-start(f32[8,512]{1,0:T(8,128)S(1)} %fusion), channel_id=1, source_target_pairs={{0,4},{1,5},{2,6},{3,7},{4,8},{5,9},{6,10},{7,11},{8,12},{9,13},{1... | collective-permute-start | bytes 49160
  1435.0 120.3 %collective-permute-start.14 = (f32[8,512]{1,0:T(8,128)S(1)}, f32[8,512]{1,0:T(8,128)S(1)}, u32[]{:S(2)}, u32[]{:S(2)}) collective-permute-start(f32[8,512]{1,0:T(8,128)S(1)} %fusion), channel_id=1, source_target_pairs={{0,3},{1,4},{2,5},{3,6},{4,7},{5,8},{6,9},{7,10},{8,11},{9,12},{10... | collective-permute-start | bytes 49160
  1448.2 107.1 %collective-permute-start.13 = (f32[8,512]{1,0:T(8,128)S(1)}, f32[8,512]{1,0:T(8,128)S(1)}, u32[]{:S(2)}, u32[]{:S(2)}) collective-permute-start(f32[8,512]{1,0:T(8,128)S(1)} %fusion), channel_id=1, source_target_pairs={{0,2},{1,3},{2,4},{3,5},{4,6},{5,7},{6,8},{7,9},{8,10},{9,11},{10,... | collective-permute-start | bytes 49160
  1461.3 94.0 %collective-permute-start.12 = (f32[8,512]{1,0:T(8,128)S(1)}, f32[8,512]{1,0:T(8,128)S(1)}, u32[]{:S(2)}, u32[]{:S(2)}) collective-permute-start(f32[8,512]{1,0:T(8,128)S(1)} %fusion), channel_id=1, source_target_pairs={{0,1},{1,2},{2,3},{3,4},{4,5},{5,6},{6,7},{7,8},{8,9},{9,10},{10,1... | collective-permute-start | bytes 49160
  (116 other events, 11485.8 us)
Sparse Core Ops, SparseCore 0:
  1063.5 258.7 all-reduce.5
where the time goes:
time: 1600 us; the launch traced here: 1590 us
  blocking collectives  735 us (46%)
  starting transfers between devices  629 us (39%)
  local copies, waits for them, and re-layouts  141 us (9%)
  matrix products  40.9 us (3%)
  other arithmetic  26.1 us (2%)
  between operations  18 us (1%)
    unnamed x1, blocking collectives  657 us
    unnamed x65, starting transfers between devices  508 us
    psum x1, blocking collectives, on_device(): lax.psum((grad_table, gain_term), ('lon', 'lat', 'lev'))  78.4 us
    ppermute x6, starting transfers between devices, extended_2(): lax.ppermute(head, axis, [((i + 1) % count, i) for i in range(ends)])  72.7 us
    ppermute x6, starting transfers between devices, extended_2(): lax.ppermute(tail, axis, [(i, (i + 1) % count) for i in range(ends)])  48.3 us
    unnamed x215, local copies, waits for them, and re-layouts  45.1 us
  transfers between devices with their start and end apart: 77, of which 0 were waited for; matrix products, arithmetic and copies ran while one was open for 6% of the time, Pallas kernels for 0%

commit v1 on v0

v1 whole, which is shorter than its diff:
```python
import jax
import jax.numpy as jnp
import numpy as np
from jax import lax
from jax.experimental import pallas as pl
from jax.experimental.pallas import tpu as pltpu
from jax.sharding import PartitionSpec as P

MESH = pl.DeviceIdType.MESH
WROWS = 6
WCOLS = 12
WCELLS = WROWS * WCOLS
WPAD = 80
EPSILON = 1e-05
NEG_FILL = 100.0
D = 512
HEADS = 8
ROWS = 12
COLS = 48
HALO_ROWS = 5
HALO_COLS = 16
EXT_ROWS = ROWS + 2 * HALO_ROWS
EXT_COLS = COLS + 2 * HALO_COLS
KBLOCKS = ROWS // WROWS + 1
MBLOCKS = COLS // WCOLS + 1
STRIP = MBLOCKS * WPAD
LAT = 8
LON = 16
LEV = 2
SMALL = 24
MB = 1024 * 1024
NT = (((1,), (1,)), ((), ()))
TN = (((0,), (0,)), ((), ()))


def mm(a, b):
    return jnp.dot(a, b, preferred_element_type=jnp.float32)


def mm_nt(a, b):
    return lax.dot_general(a, b, NT, preferred_element_type=jnp.float32)


def mm_tn(a, b):
    return lax.dot_general(a, b, TN, preferred_element_type=jnp.float32)


DIRECTIONS = [(dy, dx) for dy in (-1, 0, 1) for dx in (-1, 0, 1) if (dy, dx) != (0, 0)]
ROW_SRC = {1: (ROWS - HALO_ROWS, HALO_ROWS), 0: (0, ROWS), -1: (0, HALO_ROWS)}
ROW_DST = {1: 0, 0: HALO_ROWS, -1: HALO_ROWS + ROWS}
COL_SRC = {1: (COLS - HALO_COLS, HALO_COLS), 0: (0, COLS), -1: (0, HALO_COLS)}
COL_DST = {1: 0, 0: HALO_COLS, -1: HALO_COLS + COLS}


def halo_kernel(f_ref, c_ref, m_ref, fx_ref, cx_ref, mx_ref, send, recv, local):
    lon = lax.axis_index("lon")
    lat = lax.axis_index("lat")
    lev = lax.axis_index("lev")

    def neighbour(dy, dx):
        return (lax.rem(lon + dx + LON, LON), lax.rem(lat + dy + LAT, LAT), lev)

    barrier = pltpu.get_barrier_semaphore()
    for dy, dx in DIRECTIONS:
        pl.semaphore_signal(barrier, inc=1, device_id=neighbour(dy, dx), device_id_type=MESH)
    own = (pl.ds(HALO_ROWS, ROWS), pl.ds(HALO_COLS, COLS))
    locals_ = [
        pltpu.make_async_copy(f_ref, fx_ref.at[own[0], own[1]], local.at[0]),
        pltpu.make_async_copy(c_ref, cx_ref.at[own[0], own[1]], local.at[1]),
        pltpu.make_async_copy(m_ref, mx_ref.at[1, 1], local.at[2]),
    ]
    pl.semaphore_wait(barrier, len(DIRECTIONS))
    copies = []
    for n, (dy, dx) in enumerate(DIRECTIONS):
        rs, rn = ROW_SRC[dy]
        cs, cn = COL_SRC[dx]
        src = (pl.ds(rs, rn), pl.ds(cs, cn))
        dst = (pl.ds(ROW_DST[dy], rn), pl.ds(COL_DST[dx], cn))
        pairs = [
            (f_ref.at[src[0], src[1]], fx_ref.at[dst[0], dst[1]]),
            (c_ref.at[src[0], src[1]], cx_ref.at[dst[0], dst[1]]),
            (m_ref, mx_ref.at[1 - dy, 1 - dx]),
        ]
        for i, (a, b) in enumerate(pairs):
            copies.append(
                pltpu.make_async_remote_copy(
                    src_ref=a,
                    dst_ref=b,
                    send_sem=send.at[3 * n + i],
                    recv_sem=recv.at[3 * n + i],
                    device_id=neighbour(dy, dx),
                    device_id_type=MESH,
                )
            )
    for copy in copies:
        copy.start()
    for copy in locals_:
        copy.start()
    for copy in locals_:
        copy.wait()
    for copy in copies:
        copy.wait()


def halo(fields, cotangent, mask):
    any_spec = pl.BlockSpec(memory_space=pl.ANY)
    ext = jax.ShapeDtypeStruct((EXT_ROWS, EXT_COLS, D), jnp.bfloat16)
    return pl.pallas_call(
        halo_kernel,
        out_shape=(ext, ext, jax.ShapeDtypeStruct((3, 3, 16, 128), jnp.float32)),
        in_specs=[any_spec] * 3,
        out_specs=(any_spec,) * 3,
        scratch_shapes=[
            pltpu.SemaphoreType.DMA((24,)),
            pltpu.SemaphoreType.DMA((24,)),
            pltpu.SemaphoreType.DMA((3,)),
        ],
        compiler_params=pltpu.CompilerParams(collective_id=0, has_side_effects=True),
        name="halo_exchange",
    )(fields, cotangent, mask)


def cell_tables():
    cell = np.arange(STRIP)
    m, t = cell // WPAD, cell % WPAD
    a, b = t // WCOLS, t % WCOLS
    real = t < WCELLS
    info = np.zeros((STRIP, 4), np.int32)
    info[:, 0] = np.where(real, a * EXT_COLS + WCOLS * m + b, -100000)
    info[:, 1] = np.where(real, a, -1000)
    info[:, 2] = np.where(real, WCOLS * m + b, -1000)
    info[:, 3] = real
    lanes = np.zeros((8, STRIP), np.int32)
    lanes[0] = np.where(real, a * COLS, -100000)
    lanes[1] = np.where(real, WCOLS * m + b, -100000)
    win = np.zeros((8, WPAD), np.int32)
    t = np.arange(WPAD)
    win[0] = np.where(t < WCELLS, t // WCOLS, -1000)
    win[1] = np.where(t < WCELLS, t % WCOLS, -1000)
    perm = np.zeros((64, 64), np.float32)
    for o in range(8):
        for r in range(6):
            perm[8 * o + r, 6 * o + r] = 1
        for r in range(2):
            perm[8 * o + 6 + r, 48 + 2 * o + r] = 1
    return info, lanes, win, perm.astype(jnp.bfloat16)


def local_kernel(
    shift,
    fx_ref,
    cx_ref,
    mx_ref,
    gain_ref,
    wqkv_ref,
    wproj_ref,
    bias_ref,
    info_ref,
    lanes_ref,
    win_ref,
    perm_ref,
    out_ref,
    gf_ref,
    part_ref,
    g_ref,
    gg_ref,
    norm_s,
    mean_s,
    rstd_s,
    qkv_s,
    gm_s,
    key_s,
    mix_s,
    gc_s,
    mixo_s,
    gco_s,
):
    bf = jnp.bfloat16
    f32 = jnp.float32
    lat_shift = shift[0]
    lon_shift = shift[1]
    lat_base = shift[2]
    gain = gain_ref[...]
    g_ref[...] = jnp.zeros_like(g_ref)
    half = lax.broadcasted_iota(jnp.int32, (1, 128), 1) < 64
    lane4 = lax.broadcasted_iota(jnp.int32, (1, 256), 1)
    head_masks = [
        jnp.where((lane4 >= 64 * h) & (lane4 < 64 * h + 64), 1.0, 0.0).astype(bf) for h in range(4)
    ]

    def strip(k, carry):
        start = lat_shift - 1 + WROWS * k
        x = fx_ref[pl.ds(start, WROWS)].reshape(WROWS * EXT_COLS, D).astype(f32)
        mean = jnp.mean(x, axis=-1, keepdims=True)
        cen = x - mean
        var = jnp.mean(cen * cen, axis=-1, keepdims=True)
        rstd = lax.rsqrt(var + EPSILON)
        norm = (cen * rstd * gain).astype(bf)
        norm_s[pl.ds(WROWS * k, WROWS)] = norm.reshape(WROWS, EXT_COLS, D)
        mean_s[pl.ds(WROWS * k, WROWS)] = mean.reshape(WROWS, EXT_COLS, 1)
        rstd_s[pl.ds(WROWS * k, WROWS)] = rstd.reshape(WROWS, EXT_COLS, 1)
        acol = info_ref[:, 1:2]
        xcol = info_ref[:, 2:3] + (lon_shift + 4)
        grow = acol + (lat_shift - WROWS + WROWS * k + lat_base)
        valid = (grow >= 0) & (grow < LAT * ROWS)
        target = jnp.where(valid, info_ref[:, 0:1] + (lon_shift + 4), -1)
        lane = lax.broadcasted_iota(jnp.int32, (STRIP, WROWS * EXT_COLS), 1)
        pick = jnp.where(lane == target, 1.0, 0.0).astype(bf)
        nw = mm(pick, norm).astype(bf)
        cot = cx_ref[pl.ds(start, WROWS)].reshape(WROWS * EXT_COLS, D)
        cw = mm(pick, cot).astype(bf)
        qkv = mm_nt(nw, wqkv_ref[...]).astype(bf)
        qkv_s[:, : D] = qkv[:, : D] * jnp.asarray(0.125, bf)
        qkv_s[:, D:] = qkv[:, D:]
        gm_s[...] = mm(cw, wproj_ref[...]).astype(bf)
        lane = lax.broadcasted_iota(jnp.int32, (STRIP, 384), 1)
        mpick = (lane == xcol + 32) | (lane == xcol + 112) | (lane == xcol + 192)
        mpick = jnp.where(mpick, 1.0, 0.0).astype(bf)
        by_row = mm_nt(mpick, mx_ref[...].astype(bf))
        erow = acol + start
        flat = jnp.where(erow < 5, erow + 7, jnp.where(erow < 17, erow + 11, erow + 15))
        lane = lax.broadcasted_iota(jnp.int32, (STRIP, 48), 1)
        keep = jnp.sum(jnp.where((lane == flat) & valid, by_row, 0.0), axis=-1, keepdims=True)
        key_s[...] = jnp.where(info_ref[:, 3:4] > 0, NEG_FILL * (keep - 1.0), -1e30)
        win_row = win_ref[0:1, :] + (lat_shift - WROWS + WROWS * k)
        row_own = (win_row >= 0) & (win_row < ROWS)

        def window(m, c2):
            at = pl.multiple_of(m * WPAD, 16)
            sl = pl.ds(at, WPAD)
            key = key_s[sl, :]
            win_col = win_ref[1:2, :] + (lon_shift - WCOLS + WCOLS * m)
            own = jnp.where(row_own & (win_col >= 0) & (win_col < COLS), 1.0, 0.0)
            for q in range(2):
                lo = 256 * q
                qq = qkv_s[sl, lo : lo + 256]
                kq = qkv_s[sl, D + lo : D + lo + 256]
                vq = qkv_s[sl, 2 * D + lo : 2 * D + lo + 256]
                mq = gm_s[sl, lo : lo + 256]
                kst = jnp.concatenate([kq * h for h in head_masks], axis=0)
                vst = jnp.concatenate([vq * h for h in head_masks], axis=0)
                st = mm_nt(kst, qq).reshape(4, WPAD, WPAD)
                st = (st + bias_ref[4 * q : 4 * q + 4]) + key[None]
                top = jnp.max(st, axis=1, keepdims=True)
                ex = jnp.exp(st - top)
                pr = ex * (1.0 / jnp.sum(ex, axis=1, keepdims=True))
                prh = pr.astype(bf).reshape(4 * WPAD, WPAD)
                gp = mm_nt(vst, mq).reshape(4, WPAD, WPAD)
                pg = pr * gp
                ds = pr * (gp - jnp.sum(pg, axis=1, keepdims=True))
                g_ref[4 * q : 4 * q + 4] += ds * own[None]
                dsh = ds.astype(bf).reshape(4 * WPAD, WPAD)
                mix_s[sl, lo : lo + 256] = mm_tn(prh, vst).astype(bf)
                gc_s[sl, lo : lo + 256] = (mm_tn(dsh, kst) * 0.125).astype(bf)
                gk = mm(dsh, qq).reshape(4, WPAD, 256)
                gv = mm(prh, mq).reshape(4, WPAD, 256)
                for s, base in ((gk, D), (gv, 2 * D)):
                    for c in range(2):
                        lanes = slice(128 * c, 128 * c + 128)
                        both = jnp.where(half, s[2 * c, :, lanes], s[2 * c + 1, :, lanes])
                        gc_s[sl, base + lo + 128 * c : base + lo + 128 * c + 128] = both.astype(bf)
            return c2

        lax.fori_loop(0, MBLOCKS, window, 0)
        xl = lanes_ref[1:2, :] + (lon_shift - WCOLS)
        place = jnp.where((xl >= 0) & (xl < COLS), lanes_ref[0:1, :] + xl, -1)
        sub = lax.broadcasted_iota(jnp.int32, (WROWS * COLS, STRIP), 0)
        put = jnp.where(sub == place, 1.0, 0.0).astype(bf)
        mixo_s[pl.ds(WROWS * k, WROWS)] = mm(put, mix_s[...]).astype(bf).reshape(WROWS, COLS, D)
        gco_s[pl.ds(WROWS * k, WROWS)] = mm(put, gc_s[...]).astype(bf).reshape(WROWS, COLS, 3 * D)
        return carry

    lax.fori_loop(0, KBLOCKS, strip, 0)

    cells = ROWS * COLS
    first = pl.ds(WROWS - lat_shift, ROWS)
    own_cols = slice(HALO_COLS, HALO_COLS + COLS)
    own_rows = slice(HALO_ROWS, HALO_ROWS + ROWS)
    x = fx_ref[own_rows, own_cols, :].reshape(cells, D).astype(f32)
    cot = cx_ref[own_rows, own_cols, :].reshape(cells, D)
    norm = norm_s[first, own_cols, :].reshape(cells, D)
    mean = mean_s[first, own_cols, :].reshape(cells, 1)
    rstd = rstd_s[first, own_cols, :].reshape(cells, 1)
    mixo = mixo_s[first].reshape(cells, D)
    gco = gco_s[first].reshape(cells, 3 * D)
    out_ref[...] = (x + mm_nt(mixo, wproj_ref[...])).astype(bf).reshape(ROWS, COLS, D)
    gn = mm(gco, wqkv_ref[...])
    xhat = (x - mean) * rstd
    gg_ref[...] = jnp.sum(gn * xhat, axis=0, keepdims=True)
    gs = gn * gain
    gin = rstd * (
        gs
        - jnp.mean(gs, axis=-1, keepdims=True)
        - xhat * jnp.mean(gs * xhat, axis=-1, keepdims=True)
    )
    gf_ref[...] = (cot.astype(f32) + gin).astype(bf).reshape(ROWS, COLS, D)
    gq = mm_tn(gco, norm).astype(bf)
    gp = mm_tn(cot, mixo).astype(bf)
    for o in range(32):
        rows = jnp.concatenate([gq[48 * o : 48 * o + 48], gp[16 * o : 16 * o + 16]], axis=0)
        part_ref[64 * o : 64 * o + 64] = mm(perm_ref[...], rows).astype(bf)


def local(shift, fx, cx, mx, gain, w_qkv, w_proj, bias):
    info, lanes, win, perm = cell_tables()
    vmem = pl.BlockSpec(memory_space=pltpu.VMEM)
    smem = pl.BlockSpec(memory_space=pltpu.SMEM)
    tile = jax.ShapeDtypeStruct((ROWS, COLS, D), jnp.bfloat16)
    bf = jnp.bfloat16
    strip_rows = KBLOCKS * WROWS
    return pl.pallas_call(
        local_kernel,
        out_shape=(
            tile,
            tile,
            jax.ShapeDtypeStruct((2048, D), bf),
            jax.ShapeDtypeStruct((HEADS, WPAD, WPAD), jnp.float32),
            jax.ShapeDtypeStruct((1, D), jnp.float32),
        ),
        in_specs=[smem] + [vmem] * 11,
        out_specs=(vmem,) * 5,
        scratch_shapes=[
            pltpu.VMEM((strip_rows, EXT_COLS, D), bf),
            pltpu.VMEM((strip_rows, EXT_COLS, 1), jnp.float32),
            pltpu.VMEM((strip_rows, EXT_COLS, 1), jnp.float32),
            pltpu.VMEM((STRIP, 3 * D), bf),
            pltpu.VMEM((STRIP, D), bf),
            pltpu.VMEM((STRIP, 1), jnp.float32),
            pltpu.VMEM((STRIP, D), bf),
            pltpu.VMEM((STRIP, 3 * D), bf),
            pltpu.VMEM((strip_rows, COLS, D), bf),
            pltpu.VMEM((strip_rows, COLS, 3 * D), bf),
        ],
        compiler_params=pltpu.CompilerParams(vmem_limit_bytes=56 * MB),
        name="window_attention",
    )(
        shift, fx, cx, mx, gain, w_qkv, w_proj, bias,
        jnp.asarray(info), jnp.asarray(lanes), jnp.asarray(win), jnp.asarray(perm),
    )


PLANE = 16
ZED = 8


def reduce_kernel(
    part_ref, small_ref, rows_ref, total_ref,
    got_a, small_a, buf_b, got_b, small_b, buf_c, got_c, small_c, sum_a, sum_b,
    send_a, recv_a, send_b, recv_b, send_c, recv_c,
):
    bf = jnp.bfloat16
    f32 = jnp.float32
    lon = lax.axis_index("lon")
    lat = lax.axis_index("lat")
    lev = lax.axis_index("lev")
    zed = lon // 2
    core = lax.rem(lon, 2)
    plane = lat * 2 + lev
    sibling = (zed * 2 + (1 - core), lat, lev)

    def in_plane(p):
        return (lon, p // 2, lax.rem(p, 2))

    def along_z(z):
        return (z * 2 + core, lat, lev)

    barrier = pltpu.get_barrier_semaphore()
    pl.semaphore_signal(barrier, inc=1, device_id=sibling, device_id_type=MESH)
    for d in range(1, PLANE):
        p = lax.rem(plane + d, PLANE)
        pl.semaphore_signal(barrier, inc=1, device_id=in_plane(p), device_id_type=MESH)
    for d in range(1, ZED):
        z = lax.rem(zed + d, ZED)
        pl.semaphore_signal(barrier, inc=1, device_id=along_z(z), device_id_type=MESH)
    pl.semaphore_wait(barrier, 1 + PLANE - 1 + ZED - 1)

    def remote(src, dst, send, recv, to):
        return pltpu.make_async_remote_copy(
            src_ref=src, dst_ref=dst, send_sem=send, recv_sem=recv, device_id=to, device_id_type=MESH
        )

    copy_a = remote(part_ref.at[:, 1 - core], got_a, send_a.at[0], recv_a.at[0], sibling)
    copy_s = remote(small_ref, small_a, send_a.at[1], recv_a.at[1], sibling)
    copy_a.start()
    copy_s.start()
    copy_s.wait()
    sum_a[...] = small_ref[...] + small_a[...]
    copy_a.wait()
    for z in range(0, ZED, 2):
        lo = part_ref[z, core].astype(f32) + got_a[z].astype(f32)
        hi = part_ref[z + 1, core].astype(f32) + got_a[z + 1].astype(f32)
        both = jnp.concatenate(
            [lo.reshape(PLANE, 8, D), hi.reshape(PLANE, 8, D)], axis=1
        )
        buf_b[:, 8 * z : 8 * z + 16] = both.astype(bf)

    def copies_b(d):
        p = lax.rem(plane + d, PLANE)
        src = lax.rem(plane + (PLANE - d), PLANE)
        out = (
            remote(buf_b.at[p], got_b.at[d], send_b.at[2 * d], recv_b.at[2 * d], in_plane(p)),
            remote(sum_a, small_b.at[plane], send_b.at[2 * d + 1], recv_b.at[2 * d + 1], in_plane(p)),
        )
        return out, src

    for d in range(1, PLANE):
        for copy in copies_b(d)[0]:
            copy.start()
    acc = buf_b[plane].astype(f32)
    for d in range(1, PLANE):
        for copy in copies_b(d)[0]:
            copy.wait()
        acc = acc + got_b[d].astype(f32)
    small_b[plane] = sum_a[...]
    total = small_b[0]
    for p in range(1, PLANE):
        total = total + small_b[p]
    sum_b[...] = total

    for z in range(ZED):
        piece = acc[8 * z : 8 * z + 8]
        buf_c[z] = jnp.concatenate([piece[:, :256], piece[:, 256:]], axis=0).astype(bf)

    def copies_c(d):
        z = lax.rem(zed + d, ZED)
        return (
            remote(buf_c.at[z], got_c.at[d], send_c.at[2 * d], recv_c.at[2 * d], along_z(z)),
            remote(sum_b, small_c.at[zed], send_c.at[2 * d + 1], recv_c.at[2 * d + 1], along_z(z)),
        )

    for d in range(1, ZED):
        for copy in copies_c(d):
            copy.start()
    acc = buf_c[zed].astype(f32)
    for d in range(1, ZED):
        for copy in copies_c(d):
            copy.wait()
        acc = acc + got_c[d].astype(f32)
    rows_ref[:, :256] = acc[:8]
    rows_ref[:, 256:] = acc[8:]
    small_c[zed] = sum_b[...]
    total = small_c[0]
    for z in range(1, ZED):
        total = total + small_c[z]
    total_ref[...] = total


def reduce_all(part, small):
    vmem = pl.BlockSpec(memory_space=pltpu.VMEM)
    f32 = jnp.float32
    bf = jnp.bfloat16
    vm = pltpu.VMEM
    dma = pltpu.SemaphoreType.DMA
    return pl.pallas_call(
        reduce_kernel,
        out_shape=(
            jax.ShapeDtypeStruct((8, D), f32),
            jax.ShapeDtypeStruct((SMALL, 128), f32),
        ),
        in_specs=[vmem] * 2,
        out_specs=(vmem,) * 2,
        scratch_shapes=[
            vm((ZED, 128, D), bf),
            vm((SMALL, 128), f32),
            vm((PLANE, 64, D), bf),
            vm((PLANE, 64, D), bf),
            vm((PLANE, SMALL, 128), f32),
            vm((ZED, 16, 256), bf),
            vm((ZED, 16, 256), bf),
            vm((ZED, SMALL, 128), f32),
            vm((SMALL, 128), f32),
            vm((SMALL, 128), f32),
            dma((2,)),
            dma((2,)),
            dma((2 * PLANE,)),
            dma((2 * PLANE,)),
            dma((2 * ZED,)),
            dma((2 * ZED,)),
        ],
        compiler_params=pltpu.CompilerParams(
            collective_id=1, has_side_effects=True, vmem_limit_bytes=32 * MB
        ),
        name="reduce_gradients",
    )(part.reshape(ZED, 2, 128, D), small)


def offset_onehot():
    cell = np.arange(WPAD)
    a, b = cell // WCOLS, cell % WCOLS
    flat = (a[None, :] - a[:, None] + WROWS - 1) * (2 * WCOLS - 1) + (
        b[None, :] - b[:, None] + WCOLS - 1
    )
    real = (cell < WCELLS)[None, :] & (cell < WCELLS)[:, None]
    flat = np.where(real, flat, -1).astype(np.int32)
    entries = (2 * WROWS - 1) * (2 * WCOLS - 1)
    ids = lax.broadcasted_iota(jnp.int32, (entries, WPAD * WPAD), 0)
    return (ids == jnp.asarray(flat.reshape(1, -1))).astype(jnp.float32)


def on_device(fields, cotangent, land_mask, shift_offsets, norm_gain, w_qkv, w_proj, rel_bias):
    lat_shift = 1 + jnp.mod(shift_offsets[0], WROWS - 1)
    lon_shift = 1 + jnp.mod(shift_offsets[1], WCOLS - 1)
    shift = jnp.stack([lat_shift, lon_shift, lax.axis_index("lat") * ROWS]).astype(jnp.int32)
    mask = jnp.pad(land_mask.astype(jnp.float32), ((0, 4), (0, 80)))
    fx, cx, mx = halo(fields[0], cotangent[0], mask)
    mx = mx.transpose(0, 2, 1, 3).reshape(48, 384)
    onehot = offset_onehot()
    highest = lax.Precision.HIGHEST
    bias = jnp.dot(rel_bias.reshape(HEADS, -1), onehot, precision=highest)
    bias = bias.reshape(HEADS, WPAD, WPAD)
    out, gf, part, gsum, ggain = local(
        shift, fx, cx, mx, norm_gain.reshape(1, D), w_qkv, w_proj, bias
    )
    table = jnp.dot(gsum.reshape(HEADS, -1), onehot.T, precision=highest)
    small = jnp.concatenate([table.reshape(-1), ggain.reshape(-1)])
    entries = table.size
    small = jnp.pad(small, (0, SMALL * 128 - small.size)).reshape(SMALL, 128)
    rows, total = reduce_all(part, small)
    total = total.reshape(-1)
    return (
        out[None],
        gf[None],
        rows[:6],
        rows[6:],
        total[:entries].reshape(rel_bias.shape),
        total[entries : entries + D],
    )


def solution(mesh):
    return jax.shard_map(
        on_device,
        mesh=mesh,
        in_specs=(
            P("lev", "lat", "lon", None),
            P("lev", "lat", "lon", None),
            P("lat", "lon"),
            P(),
            P(),
            P(),
            P(),
            P(),
        ),
        out_specs=(
            P("lev", "lat", "lon", None),
            P("lev", "lat", "lon", None),
            P(("lon", "lat", "lev"), None),
            P(("lon", "lat", "lev"), None),
            P(),
            P(),
        ),
        check_vma=False,
    )
```

time: 1600 us -> 133 us (0.08)
  blocking collectives: 735 us -> 0 us
  starting transfers between devices: 629 us -> 0 us
  local copies, waits for them, and re-layouts: 141 us -> 9.41 us
  Pallas kernels: 0 us -> 114 us
  matrix products: 40.9 us -> 5.87 us
  other arithmetic: 26.1 us -> 1.36 us
    unnamed x1 -> x0, blocking collectives: 657 us -> none
    unnamed x65 -> x0, starting transfers between devices: 508 us -> none
    ppermute x12 -> x0, starting transfers between devices: 121 us -> none  [the longest x6 72.7 us: extended_2(): lax.ppermute(head, axis, [((i + 1) % count, i) for i in range(ends)])]
    pallas_call x0 -> x3, Pallas kernels: none -> 114 us  [the longest x1 45.1 us: halo(): pl.pallas_call(halo_kernel, out_shape=(ext, ext, jax.ShapeDtypeStruct((3,...]
    psum x1 -> x0, blocking collectives: 78.4 us -> none  [on_device(): lax.psum((grad_table, gain_term), ('lon', 'lat', 'lev'))]
    unnamed x215 -> x10, local copies, waits for them, and re-layouts: 45.1 us -> 2.69 us
    dot_general x14 -> x2, matrix products: 40.9 us -> 5.87 us  [the longest x1 2.94 us: on_device(): bias = jnp.dot(rel_bias.reshape(HEADS, -1), onehot, precision=highest)]
    reshape x9 -> x5, local copies, waits for them, and re-layouts: 29.2 us -> 2.63 us  [the longest x1 1.28 us: on_device(): table = jnp.dot(gsum.reshape(HEADS, -1), onehot.T, precision=highest)]
  transfers between devices with their start and end apart: 77 -> 0, of which waited for: 0 -> 0; matrix products, arithmetic and copies ran while one was open for 6% -> 0% of each run, Pallas kernels for 0% -> 0%
where the time goes in v1:
time: 133 us; the launch traced here: 132 us
  Pallas kernels  114 us (86%)
  local copies, waits for them, and re-layouts  9.41 us (7%)
  matrix products  5.87 us (4%)
  between operations  2.02 us (2%)
  other arithmetic  1.36 us (1%)
    pallas_call x1, Pallas kernels, halo(): pl.pallas_call(halo_kernel, out_shape=(ext, ext, jax.ShapeDtypeStruct((3,...  45.1 us
    pallas_call x1, Pallas kernels, local(): pl.pallas_call(local_kernel, out_shape=(tile, tile, jax.ShapeDtypeStruct(...  34.5 us
    pallas_call x1, Pallas kernels, reduce_all(): pl.pallas_call(reduce_kernel, out_shape=(jax.ShapeDtypeStruct((8, D), f32...  34.2 us
    dot_general x1, matrix products, on_device(): bias = jnp.dot(rel_bias.reshape(HEADS, -1), onehot, precision=highest)  2.94 us
    dot_general x1, matrix products, on_device(): table = jnp.dot(gsum.reshape(HEADS, -1), onehot.T, precision=highest)  2.93 us
    unnamed x10, local copies, waits for them, and re-layouts  2.69 us

profile of v1, /device:TPU:24, one launch (start us, length us, event | category | flops | bytes accessed | tf_op | source)
XLA Modules:
  0.0 132.4 jit_solution(15084569301590974897)
XLA Ops:
  0.6 1.3 fusion.4
  3.3 0.6 pad_add_fusion.shift
  3.9 0.7 convert_element_type.8
  4.6 0.6 pad.8.m_ref
  5.2 0.8 copy.21
  6.0 0.1 reshape.51
  6.1 2.9 %convolution_bitcast_fusion = f32[8,6400]{1,0:T(8,128)S(1)} fusion(f32[8,253]{1,0:T(8,128)S(1)} %reshape.51, s32[6400]{0:T(1024)} %constant.56), kind=kOutput, calls=%fused_computation | convolution fusion | flops 157062400 | bytes 238496 | tf_op jit(solution)/shard_map/dot_general | solution.py:509
  9.0 1.0 reshape.52.bias_ref
  10.0 45.1 %halo_exchange.1 = (bf16[22,80,512]{2,1,0:T(8,128)(2,1)}, bf16[22,80,512]{2,1,0:T(8,128)(2,1)}, f32[3,3,16,128]{3,2,1,0:T(8,128)}) custom-call(bf16[12,48,512]{2,1,0:T(8,128)(2,1)} %bitcast.30, bf16[12,48,512]{2,1,0:T(8,128)(2,1)} %bitcast.31, f32[16,128]{1,0:T(8,128)} %pad.8.m_ref), custom_call_target="tpu_custom_call" | custom-call | tf_op jit(solution)/shard_map/halo_exchange/pallas_call | solution.py:108
  55.0 0.9 copy.20
  56.0 0.6 copy.25
  56.6 0.0 copy-start.2
  56.6 34.5 %window_attention.1 = (bf16[12,48,512]{2,1,0:T(8,128)(2,1)}, bf16[12,48,512]{2,1,0:T(8,128)(2,1)}, bf16[2048,512]{1,0:T(8,128)(2,1)}, f32[8,80,80]{2,1,0:T(8,128)}, f32[1,512]{1,0:T(1,128)}) custom-call(s32[3]{0:T(128)} %pad_add_fusion.shift, bf16[22,80,512]{2,1,0:T(8,128)(2,1)} %get-tuple-element.16.fx_ref, bf16[22,80,512]{2,1,0:T(8,128)(2,1)} %get-tuple-element.17.cx_ref, ...), custom_call_target="tpu_custom_call" | custom-call | tf_op jit(solution)/shard_map/window_attention/pallas_call | solution.py:311
  91.1 0.0 copy-start.1
  91.1 0.0 copy-start
  91.2 1.3 reshape.54
  92.4 0.0 copy-done.2
  92.4 2.9 %fusion = f32[8,253]{1,0:T(8,128)S(1)} fusion(f32[8,6400]{1,0:T(8,128)S(1)} %reshape.54, s32[6400]{0:T(1024)S(1)} %copy-done.2), kind=kOutput, calls=%fused_computation.2 | convolution fusion | flops 157062400 | bytes 238496 | tf_op jit(solution)/shard_map/dot_general | solution.py:514
  95.4 0.2 reshape.55
  95.5 0.0 copy-done.1
  95.5 0.1 fusion.3.small_ref
  95.6 0.0 copy-done
  95.6 34.2 %reduce_gradients.1 = (f32[8,512]{1,0:T(8,128)S(1)}, f32[24,128]{1,0:T(8,128)S(1)}) custom-call(bf16[8,2,128,512]{3,2,1,0:T(8,128)(2,1)S(1)} %bitcast.26, f32[24,128]{1,0:T(8,128)S(1)} %fusion.3.small_ref), custom_call_target="tpu_custom_call" | custom-call | tf_op jit(solution)/shard_map/reduce_gradients/pallas_call | solution.py:454
  129.8 0.6 slice.25
  130.4 0.6 slice.21
  131.0 0.2 reshape.59
  131.2 0.6 copy.22
  131.8 0.6 copy.27
  (1 shorter events, 0.0 us)
Async XLA Ops:
  56.6 35.8 %copy-start.2 = (s32[6400]{0:T(1024)S(1)}, s32[6400]{0:T(1024)}, u32[]{:S(2)}) copy-start(s32[6400]{0:T(1024)} %constant.56) | copy-start | bytes 76804
  91.1 4.4 %copy-start.1 = (f32[1,512]{1,0:T(1,128)S(1)}, f32[1,512]{1,0:T(1,128)}, u32[]{:S(2)}) copy-start(f32[1,512]{1,0:T(1,128)} %get-tuple-element.23) | copy-start | bytes 6148
  91.1 4.5 %copy-start = (bf16[2048,512]{1,0:T(8,128)(2,1)S(1)}, bf16[2048,512]{1,0:T(8,128)(2,1)}, u32[]{:S(2)}) copy-start(bf16[2048,512]{1,0:T(8,128)(2,1)} %get-tuple-element.21) | copy-start | bytes 6291460

commit v2 on v1

--- a/solution.py
+++ b/solution.py
@@ -45,79 +45,12 @@
     return lax.dot_general(a, b, TN, preferred_element_type=jnp.float32)
 
 
+UP, DOWN = 0, 1
+LEFT, RIGHT = 0, 1
 DIRECTIONS = [(dy, dx) for dy in (-1, 0, 1) for dx in (-1, 0, 1) if (dy, dx) != (0, 0)]
-ROW_SRC = {1: (ROWS - HALO_ROWS, HALO_ROWS), 0: (0, ROWS), -1: (0, HALO_ROWS)}
-ROW_DST = {1: 0, 0: HALO_ROWS, -1: HALO_ROWS + ROWS}
-COL_SRC = {1: (COLS - HALO_COLS, HALO_COLS), 0: (0, COLS), -1: (0, HALO_COLS)}
-COL_DST = {1: 0, 0: HALO_COLS, -1: HALO_COLS + COLS}
-
-
-def halo_kernel(f_ref, c_ref, m_ref, fx_ref, cx_ref, mx_ref, send, recv, local):
-    lon = lax.axis_index("lon")
-    lat = lax.axis_index("lat")
-    lev = lax.axis_index("lev")
-
-    def neighbour(dy, dx):
-        return (lax.rem(lon + dx + LON, LON), lax.rem(lat + dy + LAT, LAT), lev)
-
-    barrier = pltpu.get_barrier_semaphore()
-    for dy, dx in DIRECTIONS:
-        pl.semaphore_signal(barrier, inc=1, device_id=neighbour(dy, dx), device_id_type=MESH)
-    own = (pl.ds(HALO_ROWS, ROWS), pl.ds(HALO_COLS, COLS))
-    locals_ = [
-        pltpu.make_async_copy(f_ref, fx_ref.at[own[0], own[1]], local.at[0]),
-        pltpu.make_async_copy(c_ref, cx_ref.at[own[0], own[1]], local.at[1]),
-        pltpu.make_async_copy(m_ref, mx_ref.at[1, 1], local.at[2]),
-    ]
-    pl.semaphore_wait(barrier, len(DIRECTIONS))
-    copies = []
-    for n, (dy, dx) in enumerate(DIRECTIONS):
-        rs, rn = ROW_SRC[dy]
-        cs, cn = COL_SRC[dx]
-        src = (pl.ds(rs, rn), pl.ds(cs, cn))
-        dst = (pl.ds(ROW_DST[dy], rn), pl.ds(COL_DST[dx], cn))
-        pairs = [
-            (f_ref.at[src[0], src[1]], fx_ref.at[dst[0], dst[1]]),
-            (c_ref.at[src[0], src[1]], cx_ref.at[dst[0], dst[1]]),
-            (m_ref, mx_ref.at[1 - dy, 1 - dx]),
-        ]
-        for i, (a, b) in enumerate(pairs):
-            copies.append(
-                pltpu.make_async_remote_copy(
-                    src_ref=a,
-                    dst_ref=b,
-                    send_sem=send.at[3 * n + i],
-                    recv_sem=recv.at[3 * n + i],
-                    device_id=neighbour(dy, dx),
-                    device_id_type=MESH,
-                )
-            )
-    for copy in copies:
-        copy.start()
-    for copy in locals_:
-        copy.start()
-    for copy in locals_:
-        copy.wait()
-    for copy in copies:
-        copy.wait()
-
-
-def halo(fields, cotangent, mask):
-    any_spec = pl.BlockSpec(memory_space=pl.ANY)
-    ext = jax.ShapeDtypeStruct((EXT_ROWS, EXT_COLS, D), jnp.bfloat16)
-    return pl.pallas_call(
-        halo_kernel,
-        out_shape=(ext, ext, jax.ShapeDtypeStruct((3, 3, 16, 128), jnp.float32)),
-        in_specs=[any_spec] * 3,
-        out_specs=(any_spec,) * 3,
-        scratch_shapes=[
-            pltpu.SemaphoreType.DMA((24,)),
-            pltpu.SemaphoreType.DMA((24,)),
-            pltpu.SemaphoreType.DMA((3,)),
-        ],
-        compiler_params=pltpu.CompilerParams(collective_id=0, has_side_effects=True),
-        name="halo_exchange",
-    )(fields, cotangent, mask)
+CENTRE = pl.ds(HALO_COLS, COLS)
+FLAT = 256
+OFFSETS = [(WROWS - 1) * (2 * WCOLS - 1) + WCOLS - 1 - (2 * WCOLS - 1) * (j // WCOLS) - j % WCOLS for j in range(WCELLS)]
 
 
 def cell_tables():
@@ -143,30 +76,56 @@
             perm[8 * o + r, 6 * o + r] = 1
         for r in range(2):
             perm[8 * o + 6 + r, 48 + 2 * o + r] = 1
-    return info, lanes, win, perm.astype(jnp.bfloat16)
+    base = np.where(t < WCELLS, (2 * WCOLS - 1) * (t // WCOLS) + t % WCOLS, -1)
+    obase = (np.arange(128)[:, None] == base[None, :]).astype(np.float32)
+    return info, lanes, win, perm.astype(jnp.bfloat16), obase.astype(jnp.bfloat16)
+
+
+def three_parts(x):
+    hi = x.astype(jnp.bfloat16).astype(jnp.float32)
+    rest = x - hi
+    mid = rest.astype(jnp.bfloat16).astype(jnp.float32)
+    return hi, mid, rest - mid
+
+
+def normalized(x, gain):
+    x = x.astype(jnp.float32)
+    mean = jnp.mean(x, axis=-1, keepdims=True)
+    cen = x - mean
+    rstd = lax.rsqrt(jnp.mean(cen * cen, axis=-1, keepdims=True) + EPSILON)
+    return mean, rstd, (cen * rstd * gain).astype(jnp.bfloat16)
 
 
 def local_kernel(
     shift,
-    fx_ref,
-    cx_ref,
-    mx_ref,
+    f_ref,
+    c_ref,
+    m_ref,
     gain_ref,
     wqkv_ref,
     wproj_ref,
-    bias_ref,
+    rel_ref,
     info_ref,
     lanes_ref,
     win_ref,
     perm_ref,
+    obase_ref,
     out_ref,
     gf_ref,
     part_ref,
-    g_ref,
-    gg_ref,
+    small_ref,
+    tile_s,
+    mx_s,
+    vert_s,
+    side_s,
     norm_s,
+    cot_s,
     mean_s,
     rstd_s,
+    roll_s,
+    bias_s,
+    g_s,
+    z_s,
     qkv_s,
     gm_s,
     key_s,
@@ -174,31 +133,135 @@
     gc_s,
     mixo_s,
     gco_s,
+    send,
+    recv,
 ):
     bf = jnp.bfloat16
     f32 = jnp.float32
-    lat_shift = shift[0]
-    lon_shift = shift[1]
-    lat_base = shift[2]
+    lon = lax.axis_index("lon")
+    lat = lax.axis_index("lat")
+    lev = lax.axis_index("lev")
+    lat_shift = 1 + jnp.mod(shift[0], WROWS - 1)
+    lon_shift = 1 + jnp.mod(shift[1], WCOLS - 1)
+    lat_base = lat * ROWS
+    has_above = lat > 0
+    has_below = lat < LAT - 1
+    true = lat >= 0
+
+    def neighbour(dy, dx):
+        return (lax.rem(lon + dx + LON, LON), lat + dy, lev)
+
+    def exists(dy):
+        return {-1: has_above, 0: true, 1: has_below}[dy]
+
+    def remote(src, dst, n, to):
+        return pltpu.make_async_remote_copy(
+            src_ref=src, dst_ref=dst, send_sem=send.at[n], recv_sem=recv.at[n], device_id=to, device_id_type=MESH
+        )
+
+    barrier = pltpu.get_barrier_semaphore()
+    for dy, dx in DIRECTIONS:
+
+        @pl.when(exists(dy))
+        def _(dy=dy, dx=dx):
+            pl.semaphore_signal(barrier, inc=1, device_id=neighbour(dy, dx), device_id_type=MESH)
+
+    tile_s[...] = jnp.zeros_like(tile_s)
+    tile_s[:ROWS, :COLS] = m_ref[...].astype(f32)
+    mx_s[1, 1] = tile_s[...]
+    for absent, rows in ((lat == 0, UP), (lat == LAT - 1, DOWN)):
+
+        @pl.when(absent)
+        def _(rows=rows):
+            vert_s[:, rows] = jnp.zeros_like(vert_s[:, rows])
+            for block in range(3):
+                mx_s[block, 2 * rows] = jnp.zeros((16, 128), f32)
+
+    @pl.when(has_above & has_below)
+    def _():
+        pl.semaphore_wait(barrier, 8)
+
+    @pl.when(~(has_above & has_below))
+    def _():
+        pl.semaphore_wait(barrier, 5)
+
+    masks = []
+    for n, (dy, dx) in enumerate(DIRECTIONS):
+        copy = remote(tile_s, mx_s.at[1 - dx, 1 - dy], n, neighbour(dy, dx))
+        masks.append((copy, exists(dy), exists(-dy)))
+    vertical = []
+    for way, dy, rows in ((DOWN, -1, pl.ds(0, HALO_ROWS)), (UP, 1, pl.ds(ROWS - HALO_ROWS, HALO_ROWS))):
+        for i, src in enumerate((f_ref, c_ref)):
+            copy = remote(src.at[rows], vert_s.at[i, way, :, CENTRE], 8 + 2 * way + i, neighbour(dy, 0))
+            vertical.append((copy, exists(dy), exists(-dy)))
+    for copy, sends, _ in masks + vertical:
+        pl.when(sends)(copy.start)
+    sides = []
+    for s, dx, cols in ((LEFT, 1, pl.ds(COLS - HALO_COLS, HALO_COLS)), (RIGHT, -1, pl.ds(0, HALO_COLS))):
+        for i, src in enumerate((f_ref, c_ref)):
+            copy = remote(src.at[:, cols], side_s.at[i, s], 12 + 2 * s + i, neighbour(0, dx))
+            copy.start()
+            sides.append(copy)
+    corners = []
+    for way, there in ((UP, has_above), (DOWN, has_below)):
+        for s, dx, cols, dst in (
+            (LEFT, 1, pl.ds(COLS, HALO_COLS), pl.ds(0, HALO_COLS)),
+            (RIGHT, -1, pl.ds(HALO_COLS, HALO_COLS), pl.ds(HALO_COLS + COLS, HALO_COLS)),
+        ):
+            for i in range(2):
+                n = 16 + 4 * way + 2 * s + i
+                copy = remote(vert_s.at[i, way, :, cols], vert_s.at[i, way, :, dst], n, neighbour(0, dx))
+                corners.append((copy, there))
+
     gain = gain_ref[...]
-    g_ref[...] = jnp.zeros_like(g_ref)
     half = lax.broadcasted_iota(jnp.int32, (1, 128), 1) < 64
     lane4 = lax.broadcasted_iota(jnp.int32, (1, 256), 1)
     head_masks = [
         jnp.where((lane4 >= 64 * h) & (lane4 < 64 * h + 64), 1.0, 0.0).astype(bf) for h in range(4)
     ]
-
-    def strip(k, carry):
+    g_s[...] = jnp.zeros_like(g_s)
+
+    mean, rstd, norm = normalized(f_ref[...].reshape(ROWS * COLS, D), gain)
+    mean_s[...] = mean
+    rstd_s[...] = rstd
+    own_rows = slice(HALO_ROWS, HALO_ROWS + ROWS)
+    own_cols = slice(HALO_COLS, HALO_COLS + COLS)
+    norm_s[own_rows, own_cols] = norm.reshape(ROWS, COLS, D)
+    cot_s[own_rows, own_cols] = c_ref[...]
+
+    rel3 = jnp.concatenate(three_parts(rel_ref[...]), axis=0)
+    for j in range(WCELLS):
+        roll_s[j] = pltpu.roll(rel3, (FLAT - OFFSETS[j]) % FLAT, 1)[:, :128]
+    pairs = mm(roll_s[...].reshape(WCELLS * 24, 128).astype(bf), obase_ref[...])
+    pairs = pairs.reshape(WCELLS, 24, WPAD)
+    pairs = (pairs[:, 16:24] + pairs[:, 8:16]) + pairs[:, :8]
+    bias_s[...] = jnp.zeros_like(bias_s)
+    for j in range(WCELLS):
+        bias_s[:, j, :] = pairs[j]
+
+    for copy in sides:
+        copy.wait()
+    for s, cols in ((LEFT, slice(0, HALO_COLS)), (RIGHT, slice(HALO_COLS + COLS, EXT_COLS))):
+        norm = normalized(side_s[0, s].reshape(ROWS * HALO_COLS, D), gain)[2]
+        norm_s[own_rows, cols] = norm.reshape(ROWS, HALO_COLS, D)
+        cot_s[own_rows, cols] = side_s[1, s]
+    for copy, sends, receives in masks:
+        pl.when(sends)(copy.wait_send)
+        pl.when(receives)(copy.wait_recv)
+
+    def strip(step, carry):
+        k = lax.rem(step + 1, KBLOCKS)
+
+        @pl.when(step == 1)
+        def _():
+            for copy, there in corners:
+                pl.when(there)(copy.wait)
+            for way, rows in ((UP, slice(0, HALO_ROWS)), (DOWN, slice(HALO_ROWS + ROWS, EXT_ROWS))):
+                norm = normalized(vert_s[0, way].reshape(HALO_ROWS * EXT_COLS, D), gain)[2]
+                norm_s[rows] = norm.reshape(HALO_ROWS, EXT_COLS, D)
+                cot_s[rows] = vert_s[1, way]
+
         start = lat_shift - 1 + WROWS * k
-        x = fx_ref[pl.ds(start, WROWS)].reshape(WROWS * EXT_COLS, D).astype(f32)
-        mean = jnp.mean(x, axis=-1, keepdims=True)
-        cen = x - mean
-        var = jnp.mean(cen * cen, axis=-1, keepdims=True)
-        rstd = lax.rsqrt(var + EPSILON)
-        norm = (cen * rstd * gain).astype(bf)
-        norm_s[pl.ds(WROWS * k, WROWS)] = norm.reshape(WROWS, EXT_COLS, D)
-        mean_s[pl.ds(WROWS * k, WROWS)] = mean.reshape(WROWS, EXT_COLS, 1)
-        rstd_s[pl.ds(WROWS * k, WROWS)] = rstd.reshape(WROWS, EXT_COLS, 1)
         acol = info_ref[:, 1:2]
         xcol = info_ref[:, 2:3] + (lon_shift + 4)
         grow = acol + (lat_shift - WROWS + WROWS * k + lat_base)
@@ -206,17 +269,19 @@
         target = jnp.where(valid, info_ref[:, 0:1] + (lon_shift + 4), -1)
         lane = lax.broadcasted_iota(jnp.int32, (STRIP, WROWS * EXT_COLS), 1)
         pick = jnp.where(lane == target, 1.0, 0.0).astype(bf)
+        norm = norm_s[pl.ds(start, WROWS)].reshape(WROWS * EXT_COLS, D)
         nw = mm(pick, norm).astype(bf)
-        cot = cx_ref[pl.ds(start, WROWS)].reshape(WROWS * EXT_COLS, D)
+        cot = cot_s[pl.ds(start, WROWS)].reshape(WROWS * EXT_COLS, D)
         cw = mm(pick, cot).astype(bf)
         qkv = mm_nt(nw, wqkv_ref[...]).astype(bf)
-        qkv_s[:, : D] = qkv[:, : D] * jnp.asarray(0.125, bf)
+        qkv_s[:, :D] = qkv[:, :D] * jnp.asarray(0.125, bf)
         qkv_s[:, D:] = qkv[:, D:]
         gm_s[...] = mm(cw, wproj_ref[...]).astype(bf)
-        lane = lax.broadcasted_iota(jnp.int32, (STRIP, 384), 1)
-        mpick = (lane == xcol + 32) | (lane == xcol + 112) | (lane == xcol + 192)
-        mpick = jnp.where(mpick, 1.0, 0.0).astype(bf)
-        by_row = mm_nt(mpick, mx_ref[...].astype(bf))
+        lane = lax.broadcasted_iota(jnp.int32, (STRIP, 128), 1)
+        by_row = 0.0
+        for block, offset in enumerate((32, -16, -64)):
+            mpick = jnp.where(lane == xcol + offset, 1.0, 0.0).astype(bf)
+            by_row = by_row + mm_nt(mpick, mx_s[block].reshape(48, 128).astype(bf))
         erow = acol + start
         flat = jnp.where(erow < 5, erow + 7, jnp.where(erow < 17, erow + 11, erow + 15))
         lane = lax.broadcasted_iota(jnp.int32, (STRIP, 48), 1)
@@ -226,6 +291,15 @@
         row_own = (win_row >= 0) & (win_row < ROWS)
 
         def window(m, c2):
+            @pl.when((step == 0) & (m == 2))
+            def _():
+                for copy, sends, receives in vertical:
+                    pl.when(receives)(copy.wait_recv)
+                for copy, there in corners:
+                    pl.when(there)(copy.start)
+                for copy, sends, receives in vertical:
+                    pl.when(sends)(copy.wait_send)
+
             at = pl.multiple_of(m * WPAD, 16)
             sl = pl.ds(at, WPAD)
             key = key_s[sl, :]
@@ -240,7 +314,7 @@
                 kst = jnp.concatenate([kq * h for h in head_masks], axis=0)
                 vst = jnp.concatenate([vq * h for h in head_masks], axis=0)
                 st = mm_nt(kst, qq).reshape(4, WPAD, WPAD)
-                st = (st + bias_ref[4 * q : 4 * q + 4]) + key[None]
+                st = (st + bias_s[4 * q : 4 * q + 4]) + key[None]
                 top = jnp.max(st, axis=1, keepdims=True)
                 ex = jnp.exp(st - top)
                 pr = ex * (1.0 / jnp.sum(ex, axis=1, keepdims=True))
@@ -248,7 +322,7 @@
                 gp = mm_nt(vst, mq).reshape(4, WPAD, WPAD)
                 pg = pr * gp
                 ds = pr * (gp - jnp.sum(pg, axis=1, keepdims=True))
-                g_ref[4 * q : 4 * q + 4] += ds * own[None]
+                g_s[4 * q : 4 * q + 4] += ds * own[None]
                 dsh = ds.astype(bf).reshape(4 * WPAD, WPAD)
                 mix_s[sl, lo : lo + 256] = mm_tn(prh, vst).astype(bf)
                 gc_s[sl, lo : lo + 256] = (mm_tn(dsh, kst) * 0.125).astype(bf)
@@ -274,19 +348,17 @@
 
     cells = ROWS * COLS
     first = pl.ds(WROWS - lat_shift, ROWS)
-    own_cols = slice(HALO_COLS, HALO_COLS + COLS)
-    own_rows = slice(HALO_ROWS, HALO_ROWS + ROWS)
-    x = fx_ref[own_rows, own_cols, :].reshape(cells, D).astype(f32)
-    cot = cx_ref[own_rows, own_cols, :].reshape(cells, D)
-    norm = norm_s[first, own_cols, :].reshape(cells, D)
-    mean = mean_s[first, own_cols, :].reshape(cells, 1)
-    rstd = rstd_s[first, own_cols, :].reshape(cells, 1)
+    x = f_ref[...].reshape(cells, D).astype(f32)
+    cot = c_ref[...].reshape(cells, D)
+    norm = norm_s[own_rows, own_cols].reshape(cells, D)
+    mean = mean_s[...]
+    rstd = rstd_s[...]
     mixo = mixo_s[first].reshape(cells, D)
     gco = gco_s[first].reshape(cells, 3 * D)
     out_ref[...] = (x + mm_nt(mixo, wproj_ref[...])).astype(bf).reshape(ROWS, COLS, D)
     gn = mm(gco, wqkv_ref[...])
     xhat = (x - mean) * rstd
-    gg_ref[...] = jnp.sum(gn * xhat, axis=0, keepdims=True)
+    gg = jnp.sum(gn * xhat, axis=0, keepdims=True)
     gs = gn * gain
     gin = rstd * (
         gs
@@ -300,13 +372,31 @@
         rows = jnp.concatenate([gq[48 * o : 48 * o + 48], gp[16 * o : 16 * o + 16]], axis=0)
         part_ref[64 * o : 64 * o + 64] = mm(perm_ref[...], rows).astype(bf)
 
-
-def local(shift, fx, cx, mx, gain, w_qkv, w_proj, bias):
-    info, lanes, win, perm = cell_tables()
+    small_ref[...] = jnp.zeros_like(small_ref)
+    parts = three_parts(g_s[...].reshape(HEADS * WPAD, WPAD))
+    z = mm_nt(parts[2].astype(bf), obase_ref[...]) + mm_nt(parts[1].astype(bf), obase_ref[...])
+    z = z + mm_nt(parts[0].astype(bf), obase_ref[...])
+    z_s[...] = z.reshape(HEADS, WPAD, 128)
+    zero = jnp.zeros((HEADS, 128), f32)
+    table = jnp.zeros((HEADS, FLAT), f32)
+    for j in range(WCELLS):
+        wide = jnp.concatenate([z_s[:, j, :], zero], axis=1)
+        table = table + pltpu.roll(wide, OFFSETS[j], 1)
+    small_ref[0:8, :] = table[:, :128]
+    small_ref[8:16, :] = table[:, 128:]
+    for i in range(4):
+        small_ref[16 + i : 17 + i, :] = gg[:, 128 * i : 128 * i + 128]
+
+
+def local(shift, fields, cotangent, mask, gain, w_qkv, w_proj, rel):
+    info, lanes, win, perm, obase = cell_tables()
     vmem = pl.BlockSpec(memory_space=pltpu.VMEM)
     smem = pl.BlockSpec(memory_space=pltpu.SMEM)
     tile = jax.ShapeDtypeStruct((ROWS, COLS, D), jnp.bfloat16)
     bf = jnp.bfloat16
+    f32 = jnp.float32
+    vm = pltpu.VMEM
+    dma = pltpu.SemaphoreType.DMA
     strip_rows = KBLOCKS * WROWS
     return pl.pallas_call(
         local_kernel,
@@ -314,28 +404,40 @@
             tile,
             tile,
             jax.ShapeDtypeStruct((2048, D), bf),
-            jax.ShapeDtypeStruct((HEADS, WPAD, WPAD), jnp.float32),
-            jax.ShapeDtypeStruct((1, D), jnp.float32),
+            jax.ShapeDtypeStruct((SMALL, 128), f32),
         ),
-        in_specs=[smem] + [vmem] * 11,
-        out_specs=(vmem,) * 5,
+        in_specs=[smem] + [vmem] * 12,
+        out_specs=(vmem,) * 4,
         scratch_shapes=[
-            pltpu.VMEM((strip_rows, EXT_COLS, D), bf),
-            pltpu.VMEM((strip_rows, EXT_COLS, 1), jnp.float32),
-            pltpu.VMEM((strip_rows, EXT_COLS, 1), jnp.float32),
-            pltpu.VMEM((STRIP, 3 * D), bf),
-            pltpu.VMEM((STRIP, D), bf),
-            pltpu.VMEM((STRIP, 1), jnp.float32),
-            pltpu.VMEM((STRIP, D), bf),
-            pltpu.VMEM((STRIP, 3 * D), bf),
-            pltpu.VMEM((strip_rows, COLS, D), bf),
-            pltpu.VMEM((strip_rows, COLS, 3 * D), bf),
+            vm((16, 128), f32),
+            vm((3, 3, 16, 128), f32),
+            vm((2, 2, HALO_ROWS, EXT_COLS, D), bf),
+            vm((2, 2, ROWS, HALO_COLS, D), bf),
+            vm((EXT_ROWS, EXT_COLS, D), bf),
+            vm((EXT_ROWS, EXT_COLS, D), bf),
+            vm((ROWS * COLS, 1), f32),
+            vm((ROWS * COLS, 1), f32),
+            vm((WCELLS, 24, 128), f32),
+            vm((HEADS, WPAD, WPAD), f32),
+            vm((HEADS, WPAD, WPAD), f32),
+            vm((HEADS, WPAD, 128), f32),
+            vm((STRIP, 3 * D), bf),
+            vm((STRIP, D), bf),
+            vm((STRIP, 1), f32),
+            vm((STRIP, D), bf),
+            vm((STRIP, 3 * D), bf),
+            vm((strip_rows, COLS, D), bf),
+            vm((strip_rows, COLS, 3 * D), bf),
+            dma((24,)),
+            dma((24,)),
         ],
-        compiler_params=pltpu.CompilerParams(vmem_limit_bytes=56 * MB),
+        compiler_params=pltpu.CompilerParams(
+            collective_id=0, has_side_effects=True, vmem_limit_bytes=56 * MB
+        ),
         name="window_attention",
     )(
-        shift, fx, cx, mx, gain, w_qkv, w_proj, bias,
-        jnp.asarray(info), jnp.asarray(lanes), jnp.asarray(win), jnp.asarray(perm),
+        shift, fields, cotangent, mask, gain, w_qkv, w_proj, rel,
+        jnp.asarray(info), jnp.asarray(lanes), jnp.asarray(win), jnp.asarray(perm), jnp.asarray(obase),
     )
 
 
@@ -484,46 +586,21 @@
     )(part.reshape(ZED, 2, 128, D), small)
 
 
-def offset_onehot():
-    cell = np.arange(WPAD)
-    a, b = cell // WCOLS, cell % WCOLS
-    flat = (a[None, :] - a[:, None] + WROWS - 1) * (2 * WCOLS - 1) + (
-        b[None, :] - b[:, None] + WCOLS - 1
+def on_device(fields, cotangent, land_mask, shift_offsets, norm_gain, w_qkv, w_proj, rel_bias):
+    entries = rel_bias.shape[1] * rel_bias.shape[2]
+    rel = jnp.pad(rel_bias.reshape(HEADS, entries), ((0, 0), (0, FLAT - entries)))
+    out, gf, part, small = local(
+        shift_offsets, fields[0], cotangent[0], land_mask, norm_gain.reshape(1, D), w_qkv, w_proj, rel
     )
-    real = (cell < WCELLS)[None, :] & (cell < WCELLS)[:, None]
-    flat = np.where(real, flat, -1).astype(np.int32)
-    entries = (2 * WROWS - 1) * (2 * WCOLS - 1)
-    ids = lax.broadcasted_iota(jnp.int32, (entries, WPAD * WPAD), 0)
-    return (ids == jnp.asarray(flat.reshape(1, -1))).astype(jnp.float32)
-
-
-def on_device(fields, cotangent, land_mask, shift_offsets, norm_gain, w_qkv, w_proj, rel_bias):
-    lat_shift = 1 + jnp.mod(shift_offsets[0], WROWS - 1)
-    lon_shift = 1 + jnp.mod(shift_offsets[1], WCOLS - 1)
-    shift = jnp.stack([lat_shift, lon_shift, lax.axis_index("lat") * ROWS]).astype(jnp.int32)
-    mask = jnp.pad(land_mask.astype(jnp.float32), ((0, 4), (0, 80)))
-    fx, cx, mx = halo(fields[0], cotangent[0], mask)
-    mx = mx.transpose(0, 2, 1, 3).reshape(48, 384)
-    onehot = offset_onehot()
-    highest = lax.Precision.HIGHEST
-    bias = jnp.dot(rel_bias.reshape(HEADS, -1), onehot, precision=highest)
-    bias = bias.reshape(HEADS, WPAD, WPAD)
-    out, gf, part, gsum, ggain = local(
-        shift, fx, cx, mx, norm_gain.reshape(1, D), w_qkv, w_proj, bias
-    )
-    table = jnp.dot(gsum.reshape(HEADS, -1), onehot.T, precision=highest)
-    small = jnp.concatenate([table.reshape(-1), ggain.reshape(-1)])
-    entries = table.size
-    small = jnp.pad(small, (0, SMALL * 128 - small.size)).reshape(SMALL, 128)
     rows, total = reduce_all(part, small)
-    total = total.reshape(-1)
+    table = jnp.concatenate([total[0:8], total[8:16]], axis=1)[:, :entries]
     return (
         out[None],
         gf[None],
         rows[:6],
         rows[6:],
-        total[:entries].reshape(rel_bias.shape),
-        total[entries : entries + D],
+        table.reshape(rel_bias.shape),
+        total[16:20].reshape(D),
     )
 
 

time: 133 us -> 94.1 us (0.71)
  Pallas kernels: 114 us -> 85.3 us
  matrix products: 5.87 us -> 0 us
  local copies, waits for them, and re-layouts: 9.41 us -> 7.91 us
  other arithmetic: 1.36 us -> 0.01 us
  between operations: 2.02 us -> 0.69 us
    pallas_call x1 -> x0, Pallas kernels: 45.1 us -> none  [halo(): pl.pallas_call(halo_kernel, out_shape=(ext, ext, jax.ShapeDtypeStruct((3,...]
    pallas_call x1, Pallas kernels: 34.5 us -> 52.9 us  [local(): pl.pallas_call(local_kernel, out_shape=(tile, tile, jax.ShapeDtypeStruct(...]
    dot_general x2 -> x0, matrix products: 5.87 us -> none  [the longest x1 2.94 us: on_device(): bias = jnp.dot(rel_bias.reshape(HEADS, -1), onehot, precision=highest)]
    unnamed x10 -> x13, local copies, waits for them, and re-layouts: 2.69 us -> 5.97 us
    slice x3 -> x1, local copies, waits for them, and re-layouts: 1.96 us -> 0.01 us  [on_device(): table = jnp.concatenate([total[0:8], total[8:16]], axis=1)[:, :entries]]
    reshape x5 -> x3, local copies, waits for them, and re-layouts: 2.63 us -> 0.73 us  [the longest x1 0.58 us: on_device(): total[16:20].reshape(D)]
    pallas_call x1, Pallas kernels: 34.2 us -> 32.4 us  [reduce_all(): pl.pallas_call(reduce_kernel, out_shape=(jax.ShapeDtypeStruct((8, D), f32...]
where the time goes in v2:
time: 94.1 us; the launch traced here: 93.9 us
  Pallas kernels  85.3 us (91%)
  local copies, waits for them, and re-layouts  7.91 us (8%)
    pallas_call x1, Pallas kernels, local(): pl.pallas_call(local_kernel, out_shape=(tile, tile, jax.ShapeDtypeStruct(...  52.9 us
    pallas_call x1, Pallas kernels, reduce_all(): pl.pallas_call(reduce_kernel, out_shape=(jax.ShapeDtypeStruct((8, D), f32...  32.4 us
    unnamed x13, local copies, waits for them, and re-layouts  5.97 us

profile of v2, /device:TPU:24, one launch (start us, length us, event | category | flops | bytes accessed | tf_op | source)
XLA Modules:
  0.0 93.9 jit_solution(9439113571885251727)
XLA Ops:
  0.6 0.8 copy.21
  1.4 0.1 reshape.28
  1.5 0.6 pad.4.rel_ref
  2.1 52.9 %window_attention.1 = (bf16[12,48,512]{2,1,0:T(8,128)(2,1)}, bf16[12,48,512]{2,1,0:T(8,128)(2,1)}, bf16[2048,512]{1,0:T(8,128)(2,1)}, f32[24,128]{1,0:T(8,128)}) custom-call(s32[2]{0:T(128)} %shift.1, bf16[12,48,512]{2,1,0:T(8,128)(2,1)} %bitcast.13, bf16[12,48,512]{2,1,0:T(8,128)(2,1)} %bitcast.14, s32[12,48]{1,0:T(8,128)} %m_ref.1, f32[1,512]{1,0:T(1,128)} %bitcast.15, ...), custom_call_target="tpu_custom_call" | custom-call | tf_op jit(solution)/shard_map/window_attention/pallas_call | solution.py:401
  55.0 0.0 copy-start
  55.0 1.6 %copy-done = bf16[2048,512]{1,0:T(8,128)(2,1)S(1)} copy-done((bf16[2048,512]{1,0:T(8,128)(2,1)S(1)}, bf16[2048,512]{1,0:T(8,128)(2,1)}, u32[]{:S(2)}) %copy-start) | copy-done | bytes 2097176
  56.6 0.0 copy-start.1
  56.6 0.7 copy-done.1
  57.3 0.0 copy-start.3
  57.3 0.0 copy-start.2
  57.3 32.4 %reduce_gradients.1 = (f32[8,512]{1,0:T(8,128)S(1)}, f32[24,128]{1,0:T(8,128)S(1)}) custom-call(bf16[8,2,128,512]{3,2,1,0:T(8,128)(2,1)S(1)} %bitcast.9, f32[24,128]{1,0:T(8,128)S(1)} %copy-done.1), custom_call_target="tpu_custom_call" | custom-call | tf_op jit(solution)/shard_map/reduce_gradients/pallas_call | solution.py:556
  89.7 0.1 reshape.30
  89.8 0.6 copy.22
  90.4 0.6 slice.19
  91.0 0.6 slice_bitcast_fusion
  91.6 0.0 copy-done.3
  91.6 0.8 copy.26
  92.4 0.0 copy-done.2
  92.4 0.8 copy.27
  93.3 0.6 copy.28
  (2 shorter events, 0.0 us)
Async XLA Ops:
  55.0 1.6 %copy-start = (bf16[2048,512]{1,0:T(8,128)(2,1)S(1)}, bf16[2048,512]{1,0:T(8,128)(2,1)}, u32[]{:S(2)}) copy-start(bf16[2048,512]{1,0:T(8,128)(2,1)} %get-tuple-element.14) | copy-start | bytes 6291460
  56.6 0.7 copy-start.1
  57.3 34.3 %copy-start.3 = (bf16[12,48,512]{2,1,0:T(8,128)(2,1)S(1)}, bf16[12,48,512]{2,1,0:T(8,128)(2,1)}, u32[]{:S(2)}) copy-start(bf16[12,48,512]{2,1,0:T(8,128)(2,1)} %get-tuple-element.12) | copy-start | bytes 1769476
  57.3 35.1 %copy-start.2 = (bf16[12,48,512]{2,1,0:T(8,128)(2,1)S(1)}, bf16[12,48,512]{2,1,0:T(8,128)(2,1)}, u32[]{:S(2)}) copy-start(bf16[12,48,512]{2,1,0:T(8,128)(2,1)} %get-tuple-element.13) | copy-start | bytes 1769476

commit v3 on v2

--- a/solution.py
+++ b/solution.py
@@ -27,7 +27,6 @@
 LAT = 8
 LON = 16
 LEV = 2
-SMALL = 24
 MB = 1024 * 1024
 NT = (((1,), (1,)), ((), ()))
 TN = (((0,), (0,)), ((), ()))
@@ -122,13 +121,16 @@
     cot_s,
     mean_s,
     rstd_s,
+    rel_s,
     roll_s,
     bias_s,
     g_s,
     z_s,
+    pick_s,
+    put_s,
+    key_s,
     qkv_s,
     gm_s,
-    key_s,
     mix_s,
     gc_s,
     mixo_s,
@@ -189,29 +191,39 @@
     for n, (dy, dx) in enumerate(DIRECTIONS):
         copy = remote(tile_s, mx_s.at[1 - dx, 1 - dy], n, neighbour(dy, dx))
         masks.append((copy, exists(dy), exists(-dy)))
-    vertical = []
-    for way, dy, rows in ((DOWN, -1, pl.ds(0, HALO_ROWS)), (UP, 1, pl.ds(ROWS - HALO_ROWS, HALO_ROWS))):
-        for i, src in enumerate((f_ref, c_ref)):
+    vertical = [[], []]
+    sides = [[], []]
+    corners = [[], []]
+    for i, src in enumerate((f_ref, c_ref)):
+        for way, dy, rows in (
+            (DOWN, -1, pl.ds(0, HALO_ROWS)),
+            (UP, 1, pl.ds(ROWS - HALO_ROWS, HALO_ROWS)),
+        ):
             copy = remote(src.at[rows], vert_s.at[i, way, :, CENTRE], 8 + 2 * way + i, neighbour(dy, 0))
-            vertical.append((copy, exists(dy), exists(-dy)))
-    for copy, sends, _ in masks + vertical:
-        pl.when(sends)(copy.start)
-    sides = []
-    for s, dx, cols in ((LEFT, 1, pl.ds(COLS - HALO_COLS, HALO_COLS)), (RIGHT, -1, pl.ds(0, HALO_COLS))):
-        for i, src in enumerate((f_ref, c_ref)):
-            copy = remote(src.at[:, cols], side_s.at[i, s], 12 + 2 * s + i, neighbour(0, dx))
-            copy.start()
-            sides.append(copy)
-    corners = []
-    for way, there in ((UP, has_above), (DOWN, has_below)):
-        for s, dx, cols, dst in (
-            (LEFT, 1, pl.ds(COLS, HALO_COLS), pl.ds(0, HALO_COLS)),
-            (RIGHT, -1, pl.ds(HALO_COLS, HALO_COLS), pl.ds(HALO_COLS + COLS, HALO_COLS)),
-        ):
-            for i in range(2):
+            vertical[i].append((copy, exists(dy), exists(-dy)))
+        for s, dx, cols in ((LEFT, 1, pl.ds(COLS - HALO_COLS, HALO_COLS)), (RIGHT, -1, pl.ds(0, HALO_COLS))):
+            sides[i].append(remote(src.at[:, cols], side_s.at[i, s], 12 + 2 * s + i, neighbour(0, dx)))
+        for way, there in ((UP, has_above), (DOWN, has_below)):
+            for s, dx, cols, dst in (
+                (LEFT, 1, pl.ds(COLS, HALO_COLS), pl.ds(0, HALO_COLS)),
+                (RIGHT, -1, pl.ds(HALO_COLS, HALO_COLS), pl.ds(HALO_COLS + COLS, HALO_COLS)),
+            ):
                 n = 16 + 4 * way + 2 * s + i
                 copy = remote(vert_s.at[i, way, :, cols], vert_s.at[i, way, :, dst], n, neighbour(0, dx))
-                corners.append((copy, there))
+                corners[i].append((copy, there))
+    for copy, sends, _ in masks:
+        pl.when(sends)(copy.start)
+    for i in range(2):
+        for copy, sends, _ in vertical[i]:
+            pl.when(sends)(copy.start)
+        for copy in sides[i]:
+            copy.start()
+
+    def pass_corners(i):
+        for copy, _, receives in vertical[i]:
+            pl.when(receives)(copy.wait_recv)
+        for copy, there in corners[i]:
+            pl.when(there)(copy.start)
 
     gain = gain_ref[...]
     half = lax.broadcasted_iota(jnp.int32, (1, 128), 1) < 64
@@ -229,7 +241,12 @@
     norm_s[own_rows, own_cols] = norm.reshape(ROWS, COLS, D)
     cot_s[own_rows, own_cols] = c_ref[...]
 
-    rel3 = jnp.concatenate(three_parts(rel_ref[...]), axis=0)
+    rel_s[...] = jnp.zeros_like(rel_s)
+    flat = jnp.zeros((HEADS, FLAT), f32)
+    for u in range(2 * WROWS - 1):
+        rel_s[u, :, : 2 * WCOLS - 1] = rel_ref[u]
+        flat = flat + pltpu.roll(rel_s[u], (2 * WCOLS - 1) * u, 1)
+    rel3 = jnp.concatenate(three_parts(flat), axis=0)
     for j in range(WCELLS):
         roll_s[j] = pltpu.roll(rel3, (FLAT - OFFSETS[j]) % FLAT, 1)[:, :128]
     pairs = mm(roll_s[...].reshape(WCELLS * 24, 128).astype(bf), obase_ref[...])
@@ -239,70 +256,54 @@
     for j in range(WCELLS):
         bias_s[:, j, :] = pairs[j]
 
-    for copy in sides:
-        copy.wait()
-    for s, cols in ((LEFT, slice(0, HALO_COLS)), (RIGHT, slice(HALO_COLS + COLS, EXT_COLS))):
-        norm = normalized(side_s[0, s].reshape(ROWS * HALO_COLS, D), gain)[2]
-        norm_s[own_rows, cols] = norm.reshape(ROWS, HALO_COLS, D)
-        cot_s[own_rows, cols] = side_s[1, s]
+    acol = info_ref[:, 1:2]
+    valid = []
+    for k in range(KBLOCKS):
+        grow = acol + (lat_shift - WROWS + WROWS * k + lat_base)
+        valid.append((grow >= 0) & (grow < LAT * ROWS))
+        target = jnp.where(valid[k], info_ref[:, 0:1] + (lon_shift + 4), -1)
+        lane = lax.broadcasted_iota(jnp.int32, (STRIP, WROWS * EXT_COLS), 1)
+        pick_s[k] = jnp.where(lane == target, 1.0, 0.0).astype(bf)
+    xl = lanes_ref[1:2, :] + (lon_shift - WCOLS)
+    place = jnp.where((xl >= 0) & (xl < COLS), lanes_ref[0:1, :] + xl, -1)
+    sub = lax.broadcasted_iota(jnp.int32, (WROWS * COLS, STRIP), 0)
+    put_s[...] = jnp.where(sub == place, 1.0, 0.0).astype(bf)
+
     for copy, sends, receives in masks:
         pl.when(sends)(copy.wait_send)
         pl.when(receives)(copy.wait_recv)
-
-    def strip(step, carry):
-        k = lax.rem(step + 1, KBLOCKS)
-
-        @pl.when(step == 1)
-        def _():
-            for copy, there in corners:
-                pl.when(there)(copy.wait)
-            for way, rows in ((UP, slice(0, HALO_ROWS)), (DOWN, slice(HALO_ROWS + ROWS, EXT_ROWS))):
-                norm = normalized(vert_s[0, way].reshape(HALO_ROWS * EXT_COLS, D), gain)[2]
-                norm_s[rows] = norm.reshape(HALO_ROWS, EXT_COLS, D)
-                cot_s[rows] = vert_s[1, way]
-
-        start = lat_shift - 1 + WROWS * k
-        acol = info_ref[:, 1:2]
-        xcol = info_ref[:, 2:3] + (lon_shift + 4)
-        grow = acol + (lat_shift - WROWS + WROWS * k + lat_base)
-        valid = (grow >= 0) & (grow < LAT * ROWS)
-        target = jnp.where(valid, info_ref[:, 0:1] + (lon_shift + 4), -1)
-        lane = lax.broadcasted_iota(jnp.int32, (STRIP, WROWS * EXT_COLS), 1)
-        pick = jnp.where(lane == target, 1.0, 0.0).astype(bf)
-        norm = norm_s[pl.ds(start, WROWS)].reshape(WROWS * EXT_COLS, D)
-        nw = mm(pick, norm).astype(bf)
-        cot = cot_s[pl.ds(start, WROWS)].reshape(WROWS * EXT_COLS, D)
-        cw = mm(pick, cot).astype(bf)
+    xcol = info_ref[:, 2:3] + (lon_shift + 4)
+    lane = lax.broadcasted_iota(jnp.int32, (STRIP, 128), 1)
+    by_row = 0.0
+    for block, offset in enumerate((32, -16, -64)):
+        mpick = jnp.where(lane == xcol + offset, 1.0, 0.0).astype(bf)
+        by_row = by_row + mm_nt(mpick, mx_s[block].reshape(48, 128).astype(bf))
+    lane = lax.broadcasted_iota(jnp.int32, (STRIP, 48), 1)
+    for k in range(KBLOCKS):
+        erow = acol + (lat_shift - 1 + WROWS * k)
+        flat = jnp.where(erow < 5, erow + 7, jnp.where(erow < 17, erow + 11, erow + 15))
+        keep = jnp.sum(jnp.where((lane == flat) & valid[k], by_row, 0.0), axis=-1, keepdims=True)
+        key_s[k] = jnp.where(info_ref[:, 3:4] > 0, NEG_FILL * (keep - 1.0), -1e30)
+
+    def rows_of(k):
+        return pl.ds(lat_shift - 1 + WROWS * k, WROWS)
+
+    def strip(k, between=None):
+        norm = norm_s[rows_of(k)].reshape(WROWS * EXT_COLS, D)
+        cot = cot_s[rows_of(k)].reshape(WROWS * EXT_COLS, D)
+        nw = mm(pick_s[k], norm).astype(bf)
+        cw = mm(pick_s[k], cot).astype(bf)
         qkv = mm_nt(nw, wqkv_ref[...]).astype(bf)
         qkv_s[:, :D] = qkv[:, :D] * jnp.asarray(0.125, bf)
         qkv_s[:, D:] = qkv[:, D:]
         gm_s[...] = mm(cw, wproj_ref[...]).astype(bf)
-        lane = lax.broadcasted_iota(jnp.int32, (STRIP, 128), 1)
-        by_row = 0.0
-        for block, offset in enumerate((32, -16, -64)):
-            mpick = jnp.where(lane == xcol + offset, 1.0, 0.0).astype(bf)
-            by_row = by_row + mm_nt(mpick, mx_s[block].reshape(48, 128).astype(bf))
-        erow = acol + start
-        flat = jnp.where(erow < 5, erow + 7, jnp.where(erow < 17, erow + 11, erow + 15))
-        lane = lax.broadcasted_iota(jnp.int32, (STRIP, 48), 1)
-        keep = jnp.sum(jnp.where((lane == flat) & valid, by_row, 0.0), axis=-1, keepdims=True)
-        key_s[...] = jnp.where(info_ref[:, 3:4] > 0, NEG_FILL * (keep - 1.0), -1e30)
         win_row = win_ref[0:1, :] + (lat_shift - WROWS + WROWS * k)
         row_own = (win_row >= 0) & (win_row < ROWS)
-
-        def window(m, c2):
-            @pl.when((step == 0) & (m == 2))
-            def _():
-                for copy, sends, receives in vertical:
-                    pl.when(receives)(copy.wait_recv)
-                for copy, there in corners:
-                    pl.when(there)(copy.start)
-                for copy, sends, receives in vertical:
-                    pl.when(sends)(copy.wait_send)
-
-            at = pl.multiple_of(m * WPAD, 16)
-            sl = pl.ds(at, WPAD)
-            key = key_s[sl, :]
+        for m in range(MBLOCKS):
+            if between is not None and m in between:
+                between[m]()
+            sl = slice(m * WPAD, m * WPAD + WPAD)
+            key = key_s[k, sl, :]
             win_col = win_ref[1:2, :] + (lon_shift - WCOLS + WCOLS * m)
             own = jnp.where(row_own & (win_col >= 0) & (win_col < COLS), 1.0, 0.0)
             for q in range(2):
@@ -333,18 +334,30 @@
                         lanes = slice(128 * c, 128 * c + 128)
                         both = jnp.where(half, s[2 * c, :, lanes], s[2 * c + 1, :, lanes])
                         gc_s[sl, base + lo + 128 * c : base + lo + 128 * c + 128] = both.astype(bf)
-            return c2
-
-        lax.fori_loop(0, MBLOCKS, window, 0)
-        xl = lanes_ref[1:2, :] + (lon_shift - WCOLS)
-        place = jnp.where((xl >= 0) & (xl < COLS), lanes_ref[0:1, :] + xl, -1)
-        sub = lax.broadcasted_iota(jnp.int32, (WROWS * COLS, STRIP), 0)
-        put = jnp.where(sub == place, 1.0, 0.0).astype(bf)
-        mixo_s[pl.ds(WROWS * k, WROWS)] = mm(put, mix_s[...]).astype(bf).reshape(WROWS, COLS, D)
-        gco_s[pl.ds(WROWS * k, WROWS)] = mm(put, gc_s[...]).astype(bf).reshape(WROWS, COLS, 3 * D)
-        return carry
-
-    lax.fori_loop(0, KBLOCKS, strip, 0)
+        rows = slice(WROWS * k, WROWS * k + WROWS)
+        mixo_s[rows] = mm(put_s[...], mix_s[...]).astype(bf).reshape(WROWS, COLS, D)
+        gco_s[rows] = mm(put_s[...], gc_s[...]).astype(bf).reshape(WROWS, COLS, 3 * D)
+
+    side_cols = ((LEFT, slice(0, HALO_COLS)), (RIGHT, slice(HALO_COLS + COLS, EXT_COLS)))
+    end_rows = ((UP, slice(0, HALO_ROWS)), (DOWN, slice(HALO_ROWS + ROWS, EXT_ROWS)))
+    for copy in sides[0] + sides[1]:
+        copy.wait()
+    for s, cols in side_cols:
+        norm = normalized(side_s[0, s].reshape(ROWS * HALO_COLS, D), gain)[2]
+        norm_s[own_rows, cols] = norm.reshape(ROWS, HALO_COLS, D)
+        cot_s[own_rows, cols] = side_s[1, s]
+    strip(1, {2: lambda: pass_corners(0), 4: lambda: pass_corners(1)})
+    for copy, there in corners[0] + corners[1]:
+        pl.when(there)(copy.wait)
+    for way, rows in end_rows:
+        norm = normalized(vert_s[0, way].reshape(HALO_ROWS * EXT_COLS, D), gain)[2]
+        norm_s[rows] = norm.reshape(HALO_ROWS, EXT_COLS, D)
+        cot_s[rows] = vert_s[1, way]
+    strip(0)
+    strip(2)
+    for i in range(2):
+        for copy, sends, _ in vertical[i]:
+            pl.when(sends)(copy.wait_send)
 
     cells = ROWS * COLS
     first = pl.ds(WROWS - lat_shift, ROWS)
@@ -382,10 +395,8 @@
     for j in range(WCELLS):
         wide = jnp.concatenate([z_s[:, j, :], zero], axis=1)
         table = table + pltpu.roll(wide, OFFSETS[j], 1)
-    small_ref[0:8, :] = table[:, :128]
-    small_ref[8:16, :] = table[:, 128:]
-    for i in range(4):
-        small_ref[16 + i : 17 + i, :] = gg[:, 128 * i : 128 * i + 128]
+    small_ref[0:4, :] = jnp.concatenate([table[0:4], table[4:8]], axis=1)
+    small_ref[4:5, :] = gg
 
 
 def local(shift, fields, cotangent, mask, gain, w_qkv, w_proj, rel):
@@ -404,7 +415,7 @@
             tile,
             tile,
             jax.ShapeDtypeStruct((2048, D), bf),
-            jax.ShapeDtypeStruct((SMALL, 128), f32),
+            jax.ShapeDtypeStruct((8, D), f32),
         ),
         in_specs=[smem] + [vmem] * 12,
         out_specs=(vmem,) * 4,
@@ -417,13 +428,16 @@
             vm((EXT_ROWS, EXT_COLS, D), bf),
             vm((ROWS * COLS, 1), f32),
             vm((ROWS * COLS, 1), f32),
+            vm((2 * WROWS - 1, HEADS, FLAT), f32),
             vm((WCELLS, 24, 128), f32),
             vm((HEADS, WPAD, WPAD), f32),
             vm((HEADS, WPAD, WPAD), f32),
             vm((HEADS, WPAD, 128), f32),
+            vm((KBLOCKS, STRIP, WROWS * EXT_COLS), bf),
+            vm((WROWS * COLS, STRIP), bf),
+            vm((KBLOCKS, STRIP, 1), f32),
             vm((STRIP, 3 * D), bf),
             vm((STRIP, D), bf),
-            vm((STRIP, 1), f32),
             vm((STRIP, D), bf),
             vm((STRIP, 3 * D), bf),
             vm((strip_rows, COLS, D), bf),
@@ -445,10 +459,15 @@
 ZED = 8
 
 
+def as_pair(x):
+    hi = x.astype(jnp.bfloat16).astype(jnp.float32)
+    return jnp.concatenate([hi, x - hi], axis=0).astype(jnp.bfloat16)
+
+
 def reduce_kernel(
     part_ref, small_ref, rows_ref, total_ref,
-    got_a, small_a, buf_b, got_b, small_b, buf_c, got_c, small_c, sum_a, sum_b,
-    send_a, recv_a, send_b, recv_b, send_c, recv_c,
+    own_a, got_a, small_a, buf_b, got_b, buf_c, got_c,
+    load_a, send_a, recv_a, send_b, recv_b, send_c, recv_c,
 ):
     bf = jnp.bfloat16
     f32 = jnp.float32
@@ -474,77 +493,81 @@
     for d in range(1, ZED):
         z = lax.rem(zed + d, ZED)
         pl.semaphore_signal(barrier, inc=1, device_id=along_z(z), device_id_type=MESH)
-    pl.semaphore_wait(barrier, 1 + PLANE - 1 + ZED - 1)
 
     def remote(src, dst, send, recv, to):
         return pltpu.make_async_remote_copy(
             src_ref=src, dst_ref=dst, send_sem=send, recv_sem=recv, device_id=to, device_id_type=MESH
         )
 
-    copy_a = remote(part_ref.at[:, 1 - core], got_a, send_a.at[0], recv_a.at[0], sibling)
-    copy_s = remote(small_ref, small_a, send_a.at[1], recv_a.at[1], sibling)
-    copy_a.start()
+    chunks = []
+    for c in range(4):
+        rows = pl.ds(pl.multiple_of(32 * lax.rem(plane // 4 + c, 4), 32), 32)
+        there = remote(part_ref.at[:, 1 - core, rows], got_a.at[:, rows], send_a.at[c], recv_a.at[c], sibling)
+        here = pltpu.make_async_copy(part_ref.at[:, core, rows], own_a.at[:, rows], load_a.at[c])
+        here.start()
+        chunks.append((there, here, rows))
+    pl.semaphore_wait(barrier, 1 + PLANE - 1 + ZED - 1)
+    copy_s = remote(small_ref, small_a, send_a.at[4], recv_a.at[4], sibling)
     copy_s.start()
+    for there, _, _ in chunks:
+        there.start()
     copy_s.wait()
-    sum_a[...] = small_ref[...] + small_a[...]
-    copy_a.wait()
-    for z in range(0, ZED, 2):
-        lo = part_ref[z, core].astype(f32) + got_a[z].astype(f32)
-        hi = part_ref[z + 1, core].astype(f32) + got_a[z + 1].astype(f32)
-        both = jnp.concatenate(
-            [lo.reshape(PLANE, 8, D), hi.reshape(PLANE, 8, D)], axis=1
-        )
-        buf_b[:, 8 * z : 8 * z + 16] = both.astype(bf)
-
-    def copies_b(d):
+    pair = as_pair(small_ref[...] + small_a[...])
+    for p in range(PLANE):
+        buf_b[p, 64:80] = pair
+
+    def to_plane(p):
+        return remote(buf_b.at[p], got_b.at[plane], send_b.at[p], recv_b.at[plane], in_plane(p))
+
+    for c, (there, here, rows) in enumerate(chunks):
+        here.wait()
+        there.wait()
+        base = 4 * lax.rem(plane // 4 + c, 4)
+        for z in range(0, ZED, 2):
+            lo = own_a[z, rows].astype(f32) + got_a[z, rows].astype(f32)
+            hi = own_a[z + 1, rows].astype(f32) + got_a[z + 1, rows].astype(f32)
+            both = jnp.concatenate([lo.reshape(4, 8, D), hi.reshape(4, 8, D)], axis=1)
+            buf_b[pl.ds(base, 4), 8 * z : 8 * z + 16] = both.astype(bf)
+        for e in range(4):
+            p = base + lax.rem(plane + e, 4)
+
+            @pl.when(p != plane)
+            def _(p=p):
+                to_plane(p).start()
+
+    got_b[plane, 64:80] = pair
+    acc = buf_b[plane, 0:64].astype(f32)
+    for d in range(1, PLANE):
         p = lax.rem(plane + d, PLANE)
-        src = lax.rem(plane + (PLANE - d), PLANE)
-        out = (
-            remote(buf_b.at[p], got_b.at[d], send_b.at[2 * d], recv_b.at[2 * d], in_plane(p)),
-            remote(sum_a, small_b.at[plane], send_b.at[2 * d + 1], recv_b.at[2 * d + 1], in_plane(p)),
-        )
-        return out, src
-
-    for d in range(1, PLANE):
-        for copy in copies_b(d)[0]:
-            copy.start()
-    acc = buf_b[plane].astype(f32)
-    for d in range(1, PLANE):
-        for copy in copies_b(d)[0]:
-            copy.wait()
-        acc = acc + got_b[d].astype(f32)
-    small_b[plane] = sum_a[...]
-    total = small_b[0]
-    for p in range(1, PLANE):
-        total = total + small_b[p]
-    sum_b[...] = total
+        remote(buf_b.at[p], got_b.at[p], send_b.at[p], recv_b.at[p], in_plane(p)).wait()
+        acc = acc + got_b[p, 0:64].astype(f32)
+    total = jnp.zeros((16, D), f32)
+    for p in range(PLANE):
+        total = total + got_b[p, 64:80].astype(f32)
+    pair = as_pair(total[:8] + total[8:])
 
     for z in range(ZED):
         piece = acc[8 * z : 8 * z + 8]
-        buf_c[z] = jnp.concatenate([piece[:, :256], piece[:, 256:]], axis=0).astype(bf)
-
-    def copies_c(d):
+        buf_c[z, 0:16] = jnp.concatenate([piece[:, :256], piece[:, 256:]], axis=0).astype(bf)
+        buf_c[z, 16:32] = pair[:, :256]
+        buf_c[z, 32:48] = pair[:, 256:]
+
+    def along(z):
+        return remote(buf_c.at[z], got_c.at[zed], send_c.at[z], recv_c.at[zed], along_z(z))
+
+    for d in range(1, ZED):
+        along(lax.rem(zed + d, ZED)).start()
+    got_c[zed] = buf_c[zed]
+    for d in range(1, ZED):
         z = lax.rem(zed + d, ZED)
-        return (
-            remote(buf_c.at[z], got_c.at[d], send_c.at[2 * d], recv_c.at[2 * d], along_z(z)),
-            remote(sum_b, small_c.at[zed], send_c.at[2 * d + 1], recv_c.at[2 * d + 1], along_z(z)),
-        )
-
-    for d in range(1, ZED):
-        for copy in copies_c(d):
-            copy.start()
-    acc = buf_c[zed].astype(f32)
-    for d in range(1, ZED):
-        for copy in copies_c(d):
-            copy.wait()
-        acc = acc + got_c[d].astype(f32)
-    rows_ref[:, :256] = acc[:8]
-    rows_ref[:, 256:] = acc[8:]
-    small_c[zed] = sum_b[...]
-    total = small_c[0]
+        remote(buf_c.at[z], got_c.at[z], send_c.at[z], recv_c.at[z], along_z(z)).wait()
+    total = got_c[0].astype(f32)
     for z in range(1, ZED):
-        total = total + small_c[z]
-    total_ref[...] = total
+        total = total + got_c[z].astype(f32)
+    rows_ref[:, :256] = total[0:8]
+    rows_ref[:, 256:] = total[8:16]
+    total_ref[:, :256] = total[16:24] + total[24:32]
+    total_ref[:, 256:] = total[32:40] + total[40:48]
 
 
 def reduce_all(part, small):
@@ -555,32 +578,27 @@
     dma = pltpu.SemaphoreType.DMA
     return pl.pallas_call(
         reduce_kernel,
-        out_shape=(
-            jax.ShapeDtypeStruct((8, D), f32),
-            jax.ShapeDtypeStruct((SMALL, 128), f32),
-        ),
-        in_specs=[vmem] * 2,
+        out_shape=(jax.ShapeDtypeStruct((8, D), f32), jax.ShapeDtypeStruct((8, D), f32)),
+        in_specs=[pl.BlockSpec(memory_space=pl.ANY), vmem],
         out_specs=(vmem,) * 2,
         scratch_shapes=[
             vm((ZED, 128, D), bf),
-            vm((SMALL, 128), f32),
-            vm((PLANE, 64, D), bf),
-            vm((PLANE, 64, D), bf),
-            vm((PLANE, SMALL, 128), f32),
-            vm((ZED, 16, 256), bf),
-            vm((ZED, 16, 256), bf),
-            vm((ZED, SMALL, 128), f32),
-            vm((SMALL, 128), f32),
-            vm((SMALL, 128), f32),
-            dma((2,)),
-            dma((2,)),
-            dma((2 * PLANE,)),
-            dma((2 * PLANE,)),
-            dma((2 * ZED,)),
-            dma((2 * ZED,)),
+            vm((ZED, 128, D), bf),
+            vm((8, D), f32),
+            vm((PLANE, 80, D), bf),
+            vm((PLANE, 80, D), bf),
+            vm((ZED, 48, 256), bf),
+            vm((ZED, 48, 256), bf),
+            dma((4,)),
+            dma((5,)),
+            dma((5,)),
+            dma((PLANE,)),
+            dma((PLANE,)),
+            dma((ZED,)),
+            dma((ZED,)),
         ],
         compiler_params=pltpu.CompilerParams(
-            collective_id=1, has_side_effects=True, vmem_limit_bytes=32 * MB
+            collective_id=1, has_side_effects=True, vmem_limit_bytes=60 * MB
         ),
         name="reduce_gradients",
     )(part.reshape(ZED, 2, 128, D), small)
@@ -588,19 +606,19 @@
 
 def on_device(fields, cotangent, land_mask, shift_offsets, norm_gain, w_qkv, w_proj, rel_bias):
     entries = rel_bias.shape[1] * rel_bias.shape[2]
-    rel = jnp.pad(rel_bias.reshape(HEADS, entries), ((0, 0), (0, FLAT - entries)))
+    rel = rel_bias.transpose(1, 0, 2)
     out, gf, part, small = local(
         shift_offsets, fields[0], cotangent[0], land_mask, norm_gain.reshape(1, D), w_qkv, w_proj, rel
     )
     rows, total = reduce_all(part, small)
-    table = jnp.concatenate([total[0:8], total[8:16]], axis=1)[:, :entries]
+    table = jnp.concatenate([total[0:4, :FLAT], total[0:4, FLAT:]], axis=0)[:, :entries]
     return (
         out[None],
         gf[None],
         rows[:6],
         rows[6:],
         table.reshape(rel_bias.shape),
-        total[16:20].reshape(D),
+        total[4],
     )
 
 

time: 94.1 us -> 90.4 us (0.961); the launches traced: 93.9 us -> 89 us
  Pallas kernels: 85.3 us -> 82 us
  local copies, waits for them, and re-layouts: 7.91 us -> 6.29 us
    pallas_call x1, Pallas kernels: 52.9 us -> 48.1 us  [local(): pl.pallas_call(local_kernel, out_shape=(tile, tile, jax.ShapeDtypeStruct(...]
    unnamed x13 -> x10, local copies, waits for them, and re-layouts: 5.97 us -> 2.88 us
    slice x1 -> x2, local copies, waits for them, and re-layouts: 0.01 us -> 2.02 us  [the longest x1 1.3 us: on_device(): total[4]]
    pallas_call x1, Pallas kernels: 32.4 us -> 33.9 us  [reduce_all(): pl.pallas_call(reduce_kernel, out_shape=(jax.ShapeDtypeStruct((8, D), f32...]
where the time goes in v3:
time: 90.4 us; the launch traced here: 89 us
  Pallas kernels  82 us (91%)
  local copies, waits for them, and re-layouts  6.29 us (7%)
    pallas_call x1, Pallas kernels, local(): pl.pallas_call(local_kernel, out_shape=(tile, tile, jax.ShapeDtypeStruct(...  48.1 us
    pallas_call x1, Pallas kernels, reduce_all(): pl.pallas_call(reduce_kernel, out_shape=(jax.ShapeDtypeStruct((8, D), f32...  33.9 us
    unnamed x10, local copies, waits for them, and re-layouts  2.88 us

profile of v3, /device:TPU:24, one launch (start us, length us, event | category | flops | bytes accessed | tf_op | source)
XLA Modules:
  0.0 89.0 jit_solution(8899086588006994543)
XLA Ops:
  0.6 48.1 %window_attention.1 = (bf16[12,48,512]{2,1,0:T(8,128)(2,1)}, bf16[12,48,512]{2,1,0:T(8,128)(2,1)}, bf16[2048,512]{1,0:T(8,128)(2,1)}, f32[8,512]{1,0:T(8,128)}) custom-call(s32[2]{0:T(128)} %shift.1, bf16[12,48,512]{2,1,0:T(8,128)(2,1)} %bitcast.10, bf16[12,48,512]{2,1,0:T(8,128)(2,1)} %bitcast.11, s32[12,48]{1,0:T(8,128)} %m_ref.1, f32[1,512]{1,0:T(1,128)} %bitcast.16, ...), custom_call_target="tpu_custom_call" | custom-call | tf_op jit(solution)/shard_map/window_attention/pallas_call | solution.py:412
  48.8 0.0 copy-start.1
  48.8 0.0 copy-start
  48.8 33.9 %reduce_gradients.1 = (f32[8,512]{1,0:T(8,128)}, f32[8,512]{1,0:T(8,128)}) custom-call(bf16[8,2,128,512]{3,2,1,0:T(8,128)(2,1)} %bitcast.9, f32[8,512]{1,0:T(8,128)} %get-tuple-element.15.small_ref), custom_call_target="tpu_custom_call" | custom-call | tf_op jit(solution)/shard_map/reduce_gradients/pallas_call | solution.py:579
  82.7 0.0 copy-start.2
  82.7 0.7 fusion
  83.4 0.1 reshape.23
  83.5 0.6 copy.20
  84.1 1.3 %slice.19 = f32[2,512]{1,0:T(2,128)} slice(f32[8,512]{1,0:T(8,128)} %get-tuple-element.16), slice={[6:8], [0:512]} | slice | bytes 8192 | tf_op jit(solution)/shard_map/slice | solution.py:619
  85.5 1.3 %slice.23 = f32[1,512]{1,0:T(1,128)} slice(f32[8,512]{1,0:T(8,128)} %get-tuple-element.17), slice={[4:5], [0:512]} | slice | bytes 4096 | tf_op jit(solution)/shard_map/slice | solution.py:621
  86.7 0.0 copy-done.1
  86.8 0.8 copy.24
  87.6 0.0 copy-done
  87.6 0.8 copy.25
  88.4 0.0 copy-done.2
  88.4 0.6 copy.26
  (1 shorter events, 0.0 us)
Async XLA Ops:
  48.8 38.0 %copy-start.1 = (bf16[12,48,512]{2,1,0:T(8,128)(2,1)S(1)}, bf16[12,48,512]{2,1,0:T(8,128)(2,1)}, u32[]{:S(2)}) copy-start(bf16[12,48,512]{2,1,0:T(8,128)(2,1)} %get-tuple-element.12) | copy-start | bytes 1769476
  48.8 38.8 %copy-start = (bf16[12,48,512]{2,1,0:T(8,128)(2,1)S(1)}, bf16[12,48,512]{2,1,0:T(8,128)(2,1)}, u32[]{:S(2)}) copy-start(bf16[12,48,512]{2,1,0:T(8,128)(2,1)} %get-tuple-element.13) | copy-start | bytes 1769476
  82.7 5.7 %copy-start.2 = (f32[8,512]{1,0:T(8,128)S(1)}, f32[8,512]{1,0:T(8,128)}, u32[]{:S(2)}) copy-start(f32[8,512]{1,0:T(8,128)} %get-tuple-element.16) | copy-start | bytes 49156

commit v4 on v3

--- a/solution.py
+++ b/solution.py
@@ -27,6 +27,7 @@
 LAT = 8
 LON = 16
 LEV = 2
+MAIN = 384
 MB = 1024 * 1024
 NT = (((1,), (1,)), ((), ()))
 TN = (((0,), (0,)), ((), ()))
@@ -395,8 +396,9 @@
     for j in range(WCELLS):
         wide = jnp.concatenate([z_s[:, j, :], zero], axis=1)
         table = table + pltpu.roll(wide, OFFSETS[j], 1)
-    small_ref[0:4, :] = jnp.concatenate([table[0:4], table[4:8]], axis=1)
-    small_ref[4:5, :] = gg
+    small_ref[:, :FLAT] = table
+    for i in range(4):
+        small_ref[i : i + 1, FLAT:] = gg[:, 128 * i : 128 * i + 128]
 
 
 def local(shift, fields, cotangent, mask, gain, w_qkv, w_proj, rel):
@@ -415,7 +417,7 @@
             tile,
             tile,
             jax.ShapeDtypeStruct((2048, D), bf),
-            jax.ShapeDtypeStruct((8, D), f32),
+            jax.ShapeDtypeStruct((8, MAIN), f32),
         ),
         in_specs=[smem] + [vmem] * 12,
         out_specs=(vmem,) * 4,
@@ -465,9 +467,9 @@
 
 
 def reduce_kernel(
-    part_ref, small_ref, rows_ref, total_ref,
-    own_a, got_a, small_a, buf_b, got_b, buf_c, got_c,
-    load_a, send_a, recv_a, send_b, recv_b, send_c, recv_c,
+    part_ref, small_ref, rows_ref, proj_ref, table_ref, gain_ref,
+    own_a, got_a, small_a, buf_b, got_b, buf_c, got_c, buf_z, got_z, buf_y, got_y,
+    load_a, send_a, recv_a, send_b, recv_b, send_c, recv_c, send_z, recv_z, send_y, recv_y,
 ):
     bf = jnp.bfloat16
     f32 = jnp.float32
@@ -527,7 +529,9 @@
             lo = own_a[z, rows].astype(f32) + got_a[z, rows].astype(f32)
             hi = own_a[z + 1, rows].astype(f32) + got_a[z + 1, rows].astype(f32)
             both = jnp.concatenate([lo.reshape(4, 8, D), hi.reshape(4, 8, D)], axis=1)
-            buf_b[pl.ds(base, 4), 8 * z : 8 * z + 16] = both.astype(bf)
+            buf_b[pl.ds(base, 4), 8 * z : 8 * z + 16] = both[:, :, :MAIN].astype(bf)
+            buf_z[z, rows] = lo[:, MAIN:].astype(bf)
+            buf_z[z + 1, rows] = hi[:, MAIN:].astype(bf)
         for e in range(4):
             p = base + lax.rem(plane + e, 4)
 
@@ -535,22 +539,40 @@
             def _(p=p):
                 to_plane(p).start()
 
+    for d in range(1, ZED):
+        z = lax.rem(zed + d, ZED)
+        remote(buf_z.at[z], got_z.at[zed], send_z.at[z], recv_z.at[zed], along_z(z)).start()
     got_b[plane, 64:80] = pair
+    last = buf_z[zed].astype(f32)
+    for d in range(1, ZED):
+        z = lax.rem(zed + d, ZED)
+        remote(buf_z.at[z], got_z.at[z], send_z.at[z], recv_z.at[z], along_z(z)).wait()
+        last = last + got_z[z].astype(f32)
+    buf_y[...] = last.reshape(PLANE, 8, D - MAIN)
+
+    def to_keeper(p):
+        return remote(buf_y.at[p], got_y.at[plane], send_y.at[p], recv_y.at[plane], in_plane(p))
+
+    for d in range(1, PLANE):
+        to_keeper(lax.rem(plane + d, PLANE)).start()
+
     acc = buf_b[plane, 0:64].astype(f32)
     for d in range(1, PLANE):
         p = lax.rem(plane + d, PLANE)
         remote(buf_b.at[p], got_b.at[p], send_b.at[p], recv_b.at[p], in_plane(p)).wait()
         acc = acc + got_b[p, 0:64].astype(f32)
-    total = jnp.zeros((16, D), f32)
+    total = jnp.zeros((16, MAIN), f32)
     for p in range(PLANE):
         total = total + got_b[p, 64:80].astype(f32)
     pair = as_pair(total[:8] + total[8:])
 
+    blocks = [slice(128 * i, 128 * i + 128) for i in range(3)]
     for z in range(ZED):
         piece = acc[8 * z : 8 * z + 8]
-        buf_c[z, 0:16] = jnp.concatenate([piece[:, :256], piece[:, 256:]], axis=0).astype(bf)
-        buf_c[z, 16:32] = pair[:, :256]
-        buf_c[z, 32:48] = pair[:, 256:]
+        stack = [piece[:, b] for b in blocks] + [jnp.zeros((8, 128), f32)]
+        buf_c[z, 0:32] = jnp.concatenate(stack, axis=0).astype(bf)
+        for i, b in enumerate(blocks):
+            buf_c[z, 32 + 16 * i : 48 + 16 * i] = pair[:, b]
 
     def along(z):
         return remote(buf_c.at[z], got_c.at[zed], send_c.at[z], recv_c.at[zed], along_z(z))
@@ -558,16 +580,28 @@
     for d in range(1, ZED):
         along(lax.rem(zed + d, ZED)).start()
     got_c[zed] = buf_c[zed]
+    last = buf_y[plane]
+    for d in range(1, PLANE):
+        p = lax.rem(plane + d, PLANE)
+        remote(buf_y.at[p], got_y.at[p], send_y.at[p], recv_y.at[p], in_plane(p)).wait()
+        last = last + got_y[p]
     for d in range(1, ZED):
         z = lax.rem(zed + d, ZED)
         remote(buf_c.at[z], got_c.at[z], send_c.at[z], recv_c.at[z], along_z(z)).wait()
     total = got_c[0].astype(f32)
     for z in range(1, ZED):
         total = total + got_c[z].astype(f32)
-    rows_ref[:, :256] = total[0:8]
-    rows_ref[:, 256:] = total[8:16]
-    total_ref[:, :256] = total[16:24] + total[24:32]
-    total_ref[:, 256:] = total[32:40] + total[40:48]
+    for i, b in enumerate(blocks):
+        rows_ref[:, b] = total[8 * i : 8 * i + 6]
+        proj_ref[:, b] = total[8 * i + 6 : 8 * i + 8]
+    rows_ref[:, MAIN:] = last[0:6]
+    proj_ref[:, MAIN:] = last[6:8]
+    small = [total[32 + 16 * i : 40 + 16 * i] + total[40 + 16 * i : 48 + 16 * i] for i in range(3)]
+    flat = jnp.concatenate(small[:2], axis=1)
+    for u in range(2 * WROWS - 1):
+        table_ref[u] = pltpu.roll(flat, (FLAT - (2 * WCOLS - 1) * u) % FLAT, 1)[:, : 2 * WCOLS - 1]
+    for i in range(4):
+        gain_ref[:, 128 * i : 128 * i + 128] = small[2][i : i + 1]
 
 
 def reduce_all(part, small):
@@ -578,17 +612,26 @@
     dma = pltpu.SemaphoreType.DMA
     return pl.pallas_call(
         reduce_kernel,
-        out_shape=(jax.ShapeDtypeStruct((8, D), f32), jax.ShapeDtypeStruct((8, D), f32)),
+        out_shape=(
+            jax.ShapeDtypeStruct((6, D), f32),
+            jax.ShapeDtypeStruct((2, D), f32),
+            jax.ShapeDtypeStruct((2 * WROWS - 1, HEADS, 2 * WCOLS - 1), f32),
+            jax.ShapeDtypeStruct((1, D), f32),
+        ),
         in_specs=[pl.BlockSpec(memory_space=pl.ANY), vmem],
-        out_specs=(vmem,) * 2,
+        out_specs=(vmem,) * 4,
         scratch_shapes=[
             vm((ZED, 128, D), bf),
             vm((ZED, 128, D), bf),
-            vm((8, D), f32),
-            vm((PLANE, 80, D), bf),
-            vm((PLANE, 80, D), bf),
-            vm((ZED, 48, 256), bf),
-            vm((ZED, 48, 256), bf),
+            vm((8, MAIN), f32),
+            vm((PLANE, 80, MAIN), bf),
+            vm((PLANE, 80, MAIN), bf),
+            vm((ZED, 80, 128), bf),
+            vm((ZED, 80, 128), bf),
+            vm((ZED, 128, D - MAIN), bf),
+            vm((ZED, 128, D - MAIN), bf),
+            vm((PLANE, 8, D - MAIN), f32),
+            vm((PLANE, 8, D - MAIN), f32),
             dma((4,)),
             dma((5,)),
             dma((5,)),
@@ -596,6 +639,10 @@
             dma((PLANE,)),
             dma((ZED,)),
             dma((ZED,)),
+            dma((ZED,)),
+            dma((ZED,)),
+            dma((PLANE,)),
+            dma((PLANE,)),
         ],
         compiler_params=pltpu.CompilerParams(
             collective_id=1, has_side_effects=True, vmem_limit_bytes=60 * MB
@@ -605,21 +652,12 @@
 
 
 def on_device(fields, cotangent, land_mask, shift_offsets, norm_gain, w_qkv, w_proj, rel_bias):
-    entries = rel_bias.shape[1] * rel_bias.shape[2]
     rel = rel_bias.transpose(1, 0, 2)
     out, gf, part, small = local(
         shift_offsets, fields[0], cotangent[0], land_mask, norm_gain.reshape(1, D), w_qkv, w_proj, rel
     )
-    rows, total = reduce_all(part, small)
-    table = jnp.concatenate([total[0:4, :FLAT], total[0:4, FLAT:]], axis=0)[:, :entries]
-    return (
-        out[None],
-        gf[None],
-        rows[:6],
-        rows[6:],
-        table.reshape(rel_bias.shape),
-        total[4],
-    )
+    rows, proj, table, ggain = reduce_all(part, small)
+    return (out[None], gf[None], rows, proj, table.transpose(1, 0, 2), ggain.reshape(D))
 
 
 def solution(mesh):

time: 90.4 us -> 83.2 us (0.920); the launches traced: 89 us -> 83 us
  Pallas kernels: 82 us -> 78.3 us
  local copies, waits for them, and re-layouts: 6.29 us -> 4.05 us
    pallas_call x1, Pallas kernels: 33.9 us -> 30.1 us  [reduce_all(): pl.pallas_call(reduce_kernel, out_shape=(jax.ShapeDtypeStruct((6, D), f32...]
    slice x3 -> x0, local copies, waits for them, and re-layouts: 3.33 us -> none  [the longest x1 1.31 us: on_device(): rows[6:]]
    unnamed x10 -> x18, local copies, waits for them, and re-layouts: 2.88 us -> 4.05 us
where the time goes in v4:
time: 83.2 us; the launch traced here: 83 us
  Pallas kernels  78.3 us (94%)
  local copies, waits for them, and re-layouts  4.05 us (5%)
    pallas_call x1, Pallas kernels, local(): pl.pallas_call(local_kernel, out_shape=(tile, tile, jax.ShapeDtypeStruct(...  48.2 us
    pallas_call x1, Pallas kernels, reduce_all(): pl.pallas_call(reduce_kernel, out_shape=(jax.ShapeDtypeStruct((6, D), f32...  30.1 us
    unnamed x18, local copies, waits for them, and re-layouts  4.05 us

profile of v4, /device:TPU:24, one launch (start us, length us, event | category | flops | bytes accessed | tf_op | source)
XLA Modules:
  0.0 83.0 jit_solution(5252443033614282417)
XLA Ops:
  0.6 48.2 %window_attention.1 = (bf16[12,48,512]{2,1,0:T(8,128)(2,1)}, bf16[12,48,512]{2,1,0:T(8,128)(2,1)}, bf16[2048,512]{1,0:T(8,128)(2,1)}, f32[8,384]{1,0:T(8,128)}) custom-call(s32[2]{0:T(128)} %shift.1, bf16[12,48,512]{2,1,0:T(8,128)(2,1)} %bitcast.10, bf16[12,48,512]{2,1,0:T(8,128)(2,1)} %bitcast.11, s32[12,48]{1,0:T(8,128)} %m_ref.1, f32[1,512]{1,0:T(1,128)} %bitcast.16, ...), custom_call_target="tpu_custom_call" | custom-call | tf_op jit(solution)/shard_map/window_attention/pallas_call | solution.py:414
  48.8 0.0 copy-start.1
  48.8 0.0 copy-start
  48.9 30.1 %reduce_gradients.1 = (f32[6,512]{1,0:T(8,128)}, f32[2,512]{1,0:T(2,128)}, f32[11,8,23]{2,1,0:T(8,128)}, f32[1,512]{1,0:T(1,128)}) custom-call(bf16[8,2,128,512]{3,2,1,0:T(8,128)(2,1)} %bitcast.9, f32[8,384]{1,0:T(8,128)} %get-tuple-element.17.small_ref), custom_call_target="tpu_custom_call" | custom-call | tf_op jit(solution)/shard_map/reduce_gradients/pallas_call | solution.py:613
  78.9 0.0 copy-start.3
  78.9 0.0 copy-start.4
  78.9 0.0 copy-start.2
  79.0 0.0 copy-start.5
  79.0 0.0 copy-done.1
  79.0 0.8 copy.25
  79.8 0.0 copy-done
  79.8 0.8 copy.26
  80.6 0.0 copy-done.3
  80.6 0.6 copy.27
  81.2 0.0 copy-done.4
  81.2 0.6 copy.28
  81.8 0.0 copy-done.2
  81.8 0.6 copy.29
  82.4 0.0 copy-done.5
  82.4 0.6 copy.30
Async XLA Ops:
  48.8 30.1 %copy-start.1 = (bf16[12,48,512]{2,1,0:T(8,128)(2,1)S(1)}, bf16[12,48,512]{2,1,0:T(8,128)(2,1)}, u32[]{:S(2)}) copy-start(bf16[12,48,512]{2,1,0:T(8,128)(2,1)} %get-tuple-element.14) | copy-start | bytes 1769476
  48.8 31.0 %copy-start = (bf16[12,48,512]{2,1,0:T(8,128)(2,1)S(1)}, bf16[12,48,512]{2,1,0:T(8,128)(2,1)}, u32[]{:S(2)}) copy-start(bf16[12,48,512]{2,1,0:T(8,128)(2,1)} %get-tuple-element.15) | copy-start | bytes 1769476
  78.9 1.7 %copy-start.3 = (f32[6,512]{1,0:T(8,128)S(1)}, f32[6,512]{1,0:T(8,128)}, u32[]{:S(2)}) copy-start(f32[6,512]{1,0:T(8,128)} %get-tuple-element.30) | copy-start | bytes 36868
  78.9 2.3 %copy-start.4 = (f32[2,512]{1,0:T(2,128)S(1)}, f32[2,512]{1,0:T(2,128)}, u32[]{:S(2)}) copy-start(f32[2,512]{1,0:T(2,128)} %get-tuple-element.31) | copy-start | bytes 12292
  78.9 2.9 %copy-start.2 = (f32[11,8,23]{2,1,0:T(8,128)S(1)}, f32[11,8,23]{2,1,0:T(8,128)}, u32[]{:S(2)}) copy-start(f32[11,8,23]{2,1,0:T(8,128)} %get-tuple-element.20) | copy-start | bytes 24292
  79.0 3.5 %copy-start.5 = (f32[1,512]{1,0:T(1,128)S(1)}, f32[1,512]{1,0:T(1,128)}, u32[]{:S(2)}) copy-start(f32[1,512]{1,0:T(1,128)} %get-tuple-element.21) | copy-start | bytes 6148

commit v5 on v4

--- a/solution.py
+++ b/solution.py
@@ -110,8 +110,8 @@
     win_ref,
     perm_ref,
     obase_ref,
-    out_ref,
-    gf_ref,
+    mixed_ref,
+    gn_ref,
     part_ref,
     small_ref,
     tile_s,
@@ -369,17 +369,11 @@
     rstd = rstd_s[...]
     mixo = mixo_s[first].reshape(cells, D)
     gco = gco_s[first].reshape(cells, 3 * D)
-    out_ref[...] = (x + mm_nt(mixo, wproj_ref[...])).astype(bf).reshape(ROWS, COLS, D)
+    mixed_ref[...] = mixo
     gn = mm(gco, wqkv_ref[...])
+    gn_ref[...] = gn
     xhat = (x - mean) * rstd
     gg = jnp.sum(gn * xhat, axis=0, keepdims=True)
-    gs = gn * gain
-    gin = rstd * (
-        gs
-        - jnp.mean(gs, axis=-1, keepdims=True)
-        - xhat * jnp.mean(gs * xhat, axis=-1, keepdims=True)
-    )
-    gf_ref[...] = (cot.astype(f32) + gin).astype(bf).reshape(ROWS, COLS, D)
     gq = mm_tn(gco, norm).astype(bf)
     gp = mm_tn(cot, mixo).astype(bf)
     for o in range(32):
@@ -405,7 +399,6 @@
     info, lanes, win, perm, obase = cell_tables()
     vmem = pl.BlockSpec(memory_space=pltpu.VMEM)
     smem = pl.BlockSpec(memory_space=pltpu.SMEM)
-    tile = jax.ShapeDtypeStruct((ROWS, COLS, D), jnp.bfloat16)
     bf = jnp.bfloat16
     f32 = jnp.float32
     vm = pltpu.VMEM
@@ -414,8 +407,8 @@
     return pl.pallas_call(
         local_kernel,
         out_shape=(
-            tile,
-            tile,
+            jax.ShapeDtypeStruct((ROWS * COLS, D), bf),
+            jax.ShapeDtypeStruct((ROWS * COLS, D), f32),
             jax.ShapeDtypeStruct((2048, D), bf),
             jax.ShapeDtypeStruct((8, MAIN), f32),
         ),
@@ -467,9 +460,10 @@
 
 
 def reduce_kernel(
-    part_ref, small_ref, rows_ref, proj_ref, table_ref, gain_ref,
+    part_ref, small_ref, f_ref, c_ref, mixed_ref, gn_ref, wproj_ref, norm_gain_ref,
+    rows_ref, proj_ref, table_ref, gain_ref, out_ref, gf_ref, f_s, c_s, mixed_s, gn_s, wproj_s,
     own_a, got_a, small_a, buf_b, got_b, buf_c, got_c, buf_z, got_z, buf_y, got_y,
-    load_a, send_a, recv_a, send_b, recv_b, send_c, recv_c, send_z, recv_z, send_y, recv_y,
+    load, load_a, send_a, recv_a, send_b, recv_b, send_c, recv_c, send_z, recv_z, send_y, recv_y,
 ):
     bf = jnp.bfloat16
     f32 = jnp.float32
@@ -508,6 +502,14 @@
         here = pltpu.make_async_copy(part_ref.at[:, core, rows], own_a.at[:, rows], load_a.at[c])
         here.start()
         chunks.append((there, here, rows))
+    loads = [
+        pltpu.make_async_copy(src, dst, load.at[i])
+        for i, (src, dst) in enumerate(
+            ((f_ref, f_s), (c_ref, c_s), (mixed_ref, mixed_s), (gn_ref, gn_s), (wproj_ref, wproj_s))
+        )
+    ]
+    for copy in loads:
+        copy.start()
     pl.semaphore_wait(barrier, 1 + PLANE - 1 + ZED - 1)
     copy_s = remote(small_ref, small_a, send_a.at[4], recv_a.at[4], sibling)
     copy_s.start()
@@ -543,6 +545,21 @@
         z = lax.rem(zed + d, ZED)
         remote(buf_z.at[z], got_z.at[zed], send_z.at[z], recv_z.at[zed], along_z(z)).start()
     got_b[plane, 64:80] = pair
+    for copy in loads:
+        copy.wait()
+    x = f_s[...].reshape(ROWS * COLS, D).astype(f32)
+    out_ref[...] = (x + mm_nt(mixed_s[...], wproj_s[...])).astype(bf).reshape(ROWS, COLS, D)
+    cen = x - jnp.mean(x, axis=-1, keepdims=True)
+    rstd = lax.rsqrt(jnp.mean(cen * cen, axis=-1, keepdims=True) + EPSILON)
+    xhat = cen * rstd
+    gs = gn_s[...] * norm_gain_ref[...]
+    gin = rstd * (
+        gs
+        - jnp.mean(gs, axis=-1, keepdims=True)
+        - xhat * jnp.mean(gs * xhat, axis=-1, keepdims=True)
+    )
+    cot = c_s[...].reshape(ROWS * COLS, D).astype(f32)
+    gf_ref[...] = (cot + gin).astype(bf).reshape(ROWS, COLS, D)
     last = buf_z[zed].astype(f32)
     for d in range(1, ZED):
         z = lax.rem(zed + d, ZED)
@@ -604,8 +621,9 @@
         gain_ref[:, 128 * i : 128 * i + 128] = small[2][i : i + 1]
 
 
-def reduce_all(part, small):
+def reduce_all(part, small, fields, cotangent, mixed, gn, w_proj, gain):
     vmem = pl.BlockSpec(memory_space=pltpu.VMEM)
+    hbm = pl.BlockSpec(memory_space=pl.ANY)
     f32 = jnp.float32
     bf = jnp.bfloat16
     vm = pltpu.VMEM
@@ -617,10 +635,17 @@
             jax.ShapeDtypeStruct((2, D), f32),
             jax.ShapeDtypeStruct((2 * WROWS - 1, HEADS, 2 * WCOLS - 1), f32),
             jax.ShapeDtypeStruct((1, D), f32),
+            jax.ShapeDtypeStruct((ROWS, COLS, D), bf),
+            jax.ShapeDtypeStruct((ROWS, COLS, D), bf),
         ),
-        in_specs=[pl.BlockSpec(memory_space=pl.ANY), vmem],
-        out_specs=(vmem,) * 4,
+        in_specs=[hbm, vmem, hbm, hbm, hbm, hbm, hbm, vmem],
+        out_specs=(vmem,) * 6,
         scratch_shapes=[
+            vm((ROWS, COLS, D), bf),
+            vm((ROWS, COLS, D), bf),
+            vm((ROWS * COLS, D), bf),
+            vm((ROWS * COLS, D), f32),
+            vm((D, D), bf),
             vm((ZED, 128, D), bf),
             vm((ZED, 128, D), bf),
             vm((8, MAIN), f32),
@@ -632,6 +657,7 @@
             vm((ZED, 128, D - MAIN), bf),
             vm((PLANE, 8, D - MAIN), f32),
             vm((PLANE, 8, D - MAIN), f32),
+            dma((5,)),
             dma((4,)),
             dma((5,)),
             dma((5,)),
@@ -648,15 +674,18 @@
             collective_id=1, has_side_effects=True, vmem_limit_bytes=60 * MB
         ),
         name="reduce_gradients",
-    )(part.reshape(ZED, 2, 128, D), small)
+    )(part.reshape(ZED, 2, 128, D), small, fields, cotangent, mixed, gn, w_proj, gain)
 
 
 def on_device(fields, cotangent, land_mask, shift_offsets, norm_gain, w_qkv, w_proj, rel_bias):
     rel = rel_bias.transpose(1, 0, 2)
-    out, gf, part, small = local(
-        shift_offsets, fields[0], cotangent[0], land_mask, norm_gain.reshape(1, D), w_qkv, w_proj, rel
+    gain = norm_gain.reshape(1, D)
+    mixed, gn, part, small = local(
+        shift_offsets, fields[0], cotangent[0], land_mask, gain, w_qkv, w_proj, rel
     )
-    rows, proj, table, ggain = reduce_all(part, small)
+    rows, proj, table, ggain, out, gf = reduce_all(
+        part, small, fields[0], cotangent[0], mixed, gn, w_proj, gain
+    )
     return (out[None], gf[None], rows, proj, table.transpose(1, 0, 2), ggain.reshape(D))
 
 

time: 83.2 us -> 84.2 us (1.012)
  local copies, waits for them, and re-layouts: 4.05 us -> 5.2 us
    unnamed x18 -> x16, local copies, waits for them, and re-layouts: 4.05 us -> 5.2 us
where the time goes in v5:
time: 84.2 us; the launch traced here: 84 us
  Pallas kernels  78.1 us (93%)
  local copies, waits for them, and re-layouts  5.2 us (6%)
    pallas_call x1, Pallas kernels, local(): pl.pallas_call(local_kernel, out_shape=(jax.ShapeDtypeStruct((ROWS * COLS...  47.7 us
    pallas_call x1, Pallas kernels, reduce_all(): pl.pallas_call(reduce_kernel, out_shape=(jax.ShapeDtypeStruct((6, D), f32...  30.4 us
    unnamed x16, local copies, waits for them, and re-layouts  5.2 us

profile of v5, /device:TPU:24, one launch (start us, length us, event | category | flops | bytes accessed | tf_op | source)
XLA Modules:
  0.0 84.0 jit_solution(529637474887045090)
XLA Ops:
  0.6 47.7 %window_attention.1 = (bf16[576,512]{1,0:T(8,128)(2,1)}, f32[576,512]{1,0:T(8,128)}, bf16[2048,512]{1,0:T(8,128)(2,1)}, f32[8,384]{1,0:T(8,128)}) custom-call(s32[2]{0:T(128)} %shift.1, bf16[12,48,512]{2,1,0:T(8,128)(2,1)} %bitcast.9, bf16[12,48,512]{2,1,0:T(8,128)(2,1)} %bitcast.11, s32[12,48]{1,0:T(8,128)} %m_ref.1, f32[1,512]{1,0:T(1,128)} %bitcast.18, ...), custom_call_target="tpu_custom_call" | custom-call | tf_op jit(solution)/shard_map/window_attention/pallas_call | solution.py:407
  48.3 30.4 %reduce_gradients.1 = (f32[6,512]{1,0:T(8,128)}, f32[2,512]{1,0:T(2,128)}, f32[11,8,23]{2,1,0:T(8,128)}, f32[1,512]{1,0:T(1,128)}, bf16[12,48,512]{2,1,0:T(8,128)(2,1)}, /*index=5*/bf16[12,48,512]{2,1,0:T(8,128)(2,1)}) custom-call(bf16[8,2,128,512]{3,2,1,0:T(8,128)(2,1)} %bitcast.13, f32[8,384]{1,0:T(8,128)} %get-tuple-element.17.small_ref, ...), custom_call_target="tpu_custom_call" | custom-call | tf_op jit(solution)/shard_map/reduce_gradients/pallas_call | solution.py:631
  78.7 0.0 copy-start
  78.8 0.0 copy-start.2
  78.8 0.0 copy-start.3
  78.8 0.0 copy-start.1
  78.8 0.0 copy-start.4
  78.8 2.0 %copy.25 = bf16[1,12,48,512]{3,2,1,0:T(8,128)(2,1)} copy(bf16[1,12,48,512]{3,2,1,0:T(8,128)(2,1)} %bitcast.15) | data formatting | bytes 1179648
  80.8 0.0 copy-done
  80.8 0.8 copy.26
  81.6 0.0 copy-done.2
  81.6 0.6 copy.27
  82.2 0.0 copy-done.3
  82.2 0.6 copy.28
  82.8 0.0 copy-done.1
  82.8 0.6 copy.29
  83.4 0.0 copy-done.4
  83.4 0.6 copy.30
Async XLA Ops:
  78.7 2.0 %copy-start = (bf16[12,48,512]{2,1,0:T(8,128)(2,1)S(1)}, bf16[12,48,512]{2,1,0:T(8,128)(2,1)}, u32[]{:S(2)}) copy-start(bf16[12,48,512]{2,1,0:T(8,128)(2,1)} %get-tuple-element.21) | copy-start | bytes 1769476
  78.8 2.8 %copy-start.2 = (f32[6,512]{1,0:T(8,128)S(1)}, f32[6,512]{1,0:T(8,128)}, u32[]{:S(2)}) copy-start(f32[6,512]{1,0:T(8,128)} %get-tuple-element.34) | copy-start | bytes 36868
  78.8 3.4 %copy-start.3 = (f32[2,512]{1,0:T(2,128)S(1)}, f32[2,512]{1,0:T(2,128)}, u32[]{:S(2)}) copy-start(f32[2,512]{1,0:T(2,128)} %get-tuple-element.35) | copy-start | bytes 12292
  78.8 4.0 %copy-start.1 = (f32[11,8,23]{2,1,0:T(8,128)S(1)}, f32[11,8,23]{2,1,0:T(8,128)}, u32[]{:S(2)}) copy-start(f32[11,8,23]{2,1,0:T(8,128)} %get-tuple-element.24) | copy-start | bytes 24292
  78.8 4.6 %copy-start.4 = (f32[1,512]{1,0:T(1,128)S(1)}, f32[1,512]{1,0:T(1,128)}, u32[]{:S(2)}) copy-start(f32[1,512]{1,0:T(1,128)} %get-tuple-element.25) | copy-start | bytes 6148
